TPU v7x, 32 devices: a whole 2x2x4 slice. The times are simulated.
32 devices in a mesh: groups: 2 (over y), blk: 8 (over z, x), proj: 2 (over core).
Axes of the slice: x: 2, y: 2, z: 4, core: 2. Of those that a mesh axis runs over, the one named last changes fastest.
Arguments:
- documents: bfloat16 [6144, 8192], P(('groups', 'blk'), 'proj'), parts along dimension 0, may hold values from -60 to 60
- queries: bfloat16 [192, 8192], P(('groups', 'blk'), 'proj'), parts along dimension 0, may hold values from -60 to 60
- preconditioner: float32 [8192], P('proj'), may hold values from 0.1 to 3
Outputs:
- scores: float32 [6144, 96], P(('groups', 'blk', 'proj')), parts along dimension 0
There are 2 independent parts, one for each index of `groups`. A program takes and returns all parts, laid end to end along the dimension named above; an argument that names none is the same for every part. Nothing has to cross between parts.
All inputs are finite; a program needn't handle non-finite values.
Results may differ from a plain program's by a relative error of at most 0.009.
Values may be sent and summed in bfloat16 or wider, within the bound.
No kernel may reach another device: no remote copies, remote signals or barrier semaphores. Data moves between devices by JAX's collectives and lax.ppermute only.
A program may use at most 128 MiB of HBM per device.

v0:
```python
import math

import jax
import jax.numpy as jnp
from jax import lax
from jax.sharding import PartitionSpec as P

PROJ = 8192


def make_folder(doc_block, totals, pieces, offset):
    raw_scores, all_scales = totals
    query_piece, piece_scales = pieces
    partial_value = lax.dot_general(
        doc_block, query_piece, (((1,), (1,)), ((), ())), preferred_element_type=jnp.float32
    )
    raw_scores = partial_value
    all_scales = lax.dynamic_update_slice_in_dim(all_scales, piece_scales, offset, 0)
    return (raw_scores, all_scales)


def on_device(documents, queries, preconditioner):
    weighted = (queries.astype(jnp.float32) * preconditioner[None, :]).astype(jnp.bfloat16)
    doc_squares = jnp.einsum("dp,dp->d", documents, documents, preferred_element_type=jnp.float32)
    query_squares = jnp.einsum("qp,qp->q", weighted, weighted, preferred_element_type=jnp.float32)
    doc_squares, query_squares = lax.psum((doc_squares, query_squares), "proj")
    doc_scale = lax.rsqrt(doc_squares / PROJ + 1e-06)
    query_scale = lax.rsqrt(query_squares / PROJ + 1e-06)
    half_rows = documents.shape[0] // lax.axis_size("proj")
    first_row = lax.axis_index("proj") * half_rows
    total_queries = weighted.shape[0] * lax.axis_size("blk")
    my_doc_scale = lax.dynamic_slice_in_dim(doc_scale, first_row, half_rows, 0)
    own_documents = lax.all_to_all(documents, "proj", split_axis=0, concat_axis=1, tiled=True)
    widened = lax.all_gather(weighted, "proj", axis=1, tiled=True)
    initial = (
        jnp.zeros((half_rows, total_queries), jnp.float32),
        jnp.zeros((total_queries,), jnp.float32),
    )
    my_scores, all_scales = make_folder(
        own_documents,
        initial,
        (
            lax.all_gather(widened, "blk", axis=0, tiled=True),
            lax.all_gather(query_scale.astype(jnp.bfloat16), "blk", axis=0, tiled=True).astype(
                jnp.float32
            ),
        ),
        jnp.int32(0),
    )
    return my_scores * my_doc_scale[:, None] * all_scales[None, :] / math.sqrt(PROJ)


def solution(mesh):
    placed = (P(("groups", "blk"), "proj"), P(("groups", "blk"), "proj"), P("proj"))
    return jax.shard_map(
        on_device,
        mesh=mesh,
        in_specs=placed,
        out_specs=P(("groups", "blk", "proj"), None),
        check_vma=False,
    )
```

profile of v0, /device:TPU:0, one launch (start us, length us, event | category | flops | bytes accessed | tf_op | source)
XLA Modules:
  0.0 74.8 jit_solution(16817878231180142272)
XLA Ops:
  6.5 0.0 all-gather.3.cloned.1.call-start
  6.5 1.1 %fusion.4 = (f32[12]{0:T(128)S(1)}, bf16[12,4096]{1,0:T(8,128)(2,1)S(1)}) fusion(f32[4096]{0:T(1024)} %param.5, bf16[12,4096]{1,0:T(8,128)(2,1)} %param.4), kind=kLoop, calls=%fused_computation.7 | loop fusion | flops 294900 | bytes 213040 | tf_op jit(solution)/shard_map/qp,qp->q/dot_general | solution.py:25
  7.6 2.2 %all_gather.9 = bf16[12,8192]{1,0:T(8,128)(2,1)} all-gather(bf16[12,4096]{1,0:T(8,128)(2,1)S(1)} %get-tuple-element.8), channel_id=1, replica_groups=mesh['groups'=2,'blk'=8,'proj'=2] {'proj'}, dimensions={1}, use_global_device_ids=true | all-gather | bytes 294912 | tf_op jit(solution)/shard_map/all_gather | solution.py:34
  9.8 0.0 all-gather.3.cloned.1.call-update
  9.9 0.0 copy-start
  9.9 5.5 %all-to-all-start = ((bf16[2,192,4096]{2,1,0:T(8,128)(2,1)}), bf16[2,192,4096]{2,1,0:T(8,128)(2,1)}, u32[]{:S(2)}, u32[]{:S(2)}) async-start(bf16[2,192,4096]{2,1,0:T(8,128)(2,1)} %bitcast.10), calls=%async_computation | async-start | bytes 6291456 | tf_op jit(solution)/shard_map/all_to_all | solution.py:33
  15.3 0.0 copy-done
  15.4 0.7 fusion
  16.1 2.7 %all-reduce.1 = (f32[12]{0:T(128)S(1)}, f32[384]{0:T(512)S(1)}) all-reduce(f32[12]{0:T(128)S(1)} %get-tuple-element.7, f32[384]{0:T(512)S(1)} %fusion), channel_id=1, replica_groups=mesh['groups'=2,'blk'=8,'proj'=2] {'proj'}, use_global_device_ids=true, to_apply=%region_1.0 | all-reduce | flops 396 | bytes 3168 | tf_op jit(solution)/shard_map/psum | solution.py:26
  18.8 0.3 all-to-all-done
  19.1 0.0 copy-start.1
  19.1 2.2 %copy.17 = bf16[2,24,8,4096]{3,2,0,1:T(8,128)(2,1)S(1)} copy(bf16[2,24,8,4096]{3,2,1,0:T(8,128)(2,1)} %bitcast.5) | data formatting | bytes 6291456 | tf_op jit(solution)/shard_map/all_to_all | solution.py:33
  21.3 0.0 copy-done.1
  21.3 0.6 dynamic-slice
  22.6 0.2 dynamic-update-slice
  22.8 23.1 %all-reduce = bf16[96]{0:T(256)(128)(2,1)S(1)} all-reduce(bf16[96]{0:T(256)(128)(2,1)S(1)} %dynamic-update-slice), channel_id=1, replica_groups=mesh['groups'=2,'blk'=8,'proj'=2] {'blk'}, use_global_device_ids=true, to_apply=%add | all-reduce | flops 96 | bytes 384
  45.9 0.1 dynamic_slice.3
  46.0 16.0 %all-gather.3.cloned.1.call-done = bf16[8,12,8192]{2,1,0:T(8,128)(2,1)} async-done(((bf16[1,12,8192]{2,1,0:T(8,128)(2,1)}), bf16[8,12,8192]{2,1,0:T(8,128)(2,1)}) %all-gather.3.cloned.1.call-update) | async-done | bytes 1572880 | tf_op jit(solution)/shard_map/all_gather | solution.py:43
  62.0 2.6 %reshape.10 = bf16[96,8192]{1,0:T(8,128)(2,1)} reshape(bf16[8,12,8192]{2,1,0:T(8,128)(2,1)} %all-gather.3.cloned.1.call-done) | data formatting | bytes 3145728
  64.6 2.6 %fusion.3 = f32[192,96]{0,1:T(8,128)S(1)} fusion(bf16[96,8192]{1,0:T(8,128)(2,1)} %reshape.10, bf16[192,8192]{1,0:T(8,128)(2,1)S(1)} %bitcast.11, f32[96]{0:T(128)S(1)} %convert_element_type.15, f32[192]{0:T(256)S(1)} %dynamic_slice.3), kind=kOutput, calls=%fused_computation.5 | convolution fusion | flops 302045184 | bytes 4793472 | tf_op jit(solution)/shard_map/dot_general | solution.py:14
  67.2 0.7 copy.8
  (4 shorter events, 0.0 us)
Async XLA Ops:
  6.5 55.4 %all-gather.3.cloned.1.call-start = ((), (), s32[]{:S(2)}) async-start(), calls=%async_computation.1 | async-start | bytes 2359296 | tf_op jit(solution)/shard_map/all_gather | solution.py:43
  9.9 5.5 %copy-start = (bf16[384,4096]{1,0:T(8,128)(2,1)S(1)}, bf16[384,4096]{1,0:T(8,128)(2,1)}, u32[]{:S(2)}) copy-start(bf16[384,4096]{1,0:T(8,128)(2,1)} %param.3) | copy-start | bytes 9437188
  9.9 9.2 %all-to-all-start = ((bf16[2,192,4096]{2,1,0:T(8,128)(2,1)}), bf16[2,192,4096]{2,1,0:T(8,128)(2,1)}, u32[]{:S(2)}, u32[]{:S(2)}) async-start(bf16[2,192,4096]{2,1,0:T(8,128)(2,1)} %bitcast.10), calls=%async_computation | async-start | bytes 6291456 | tf_op jit(solution)/shard_map/all_to_all | solution.py:33
  19.1 2.2 %copy-start.1 = (u32[32]{0:T(128)S(1)}, u32[32]{0:T(128)}, u32[]{:S(2)}) copy-start(u32[32]{0:T(128)} %constant.24) | copy-start | bytes 388
Sparse Core Ops, SparseCore 0:
  10.0 51.9 all-gather.2
where the time goes:
time: 75.1 us; the launch traced here: 74.8 us
  blocking collectives  28 us (37%)
  waiting for transfers between devices  16.3 us (22%)
  between operations  14.1 us (19%)
  local copies, waits for them, and re-layouts  6.54 us (9%)
  starting transfers between devices  5.48 us (7%)
  matrix products  2.56 us (3%)
  other arithmetic  1.79 us (2%)
    unnamed x1, blocking collectives  23.1 us
    all_gather x1, waiting for transfers between devices, on_device(): lax.all_gather(widened, 'blk', axis=0, tiled=True)  16 us
    all_to_all x1, starting transfers between devices, on_device(): lax.all_to_all(documents, 'proj', split_axis=0, concat_axis=1, tiled=True)  5.48 us
    unnamed x8, local copies, waits for them, and re-layouts  3.49 us
    psum x1, blocking collectives, on_device(): doc_squares, query_squares = lax.psum((doc_squares, query_squares), 'proj')  2.7 us
    dot_general x1, matrix products, make_folder(): lax.dot_general(doc_block, query_piece, (((1,), (1,)), ((), ())), preferr...  2.56 us
    all_to_all x1, local copies, waits for them, and re-layouts, on_device(): lax.all_to_all(documents, 'proj', split_axis=0, concat_axis=1, tiled=True)  2.23 us
    all_gather x1, blocking collectives, on_device(): widened = lax.all_gather(weighted, 'proj', axis=1, tiled=True)  2.21 us
  transfers between devices with their start and end apart: 2, of which 2 were waited for; matrix products, arithmetic and copies ran while one was open for 5% of the time, Pallas kernels for 0%

commit v1 on v0

v1 whole, which is shorter than its diff:
```python
import functools
import math

import jax
import jax.numpy as jnp
from jax import lax
from jax.experimental import pallas as pl
from jax.experimental.pallas import tpu as pltpu
from jax.sharding import PartitionSpec as P

EPS = 1e-06
VMEM_LIMIT = 24 * 1024 * 1024
BOTH = ("blk", "proj")
NT = (((1,), (1,)), ((), ()))


def params():
    return pltpu.CompilerParams(vmem_limit_bytes=VMEM_LIMIT)


def vmem():
    return pl.BlockSpec(memory_space=pltpu.VMEM)


def smem():
    return pl.BlockSpec(memory_space=pltpu.SMEM)


def pack_kernel(queries, preconditioner, packed):
    width = packed.shape[1]
    third = width // 3
    weighted = queries[...].astype(jnp.float32) * preconditioner[...]
    tail = jnp.concatenate([weighted[4 * k : 4 * k + 4, width:] for k in range(3)], axis=1)
    packed[...] = jnp.concatenate([weighted[:, :width], tail], axis=0).astype(packed.dtype)


def unpack(packed):
    width = packed.shape[1]
    third = width // 3
    wide = packed.astype(jnp.float32)
    tail = jnp.concatenate(
        [wide[12:16, k * third : (k + 1) * third] for k in range(3)]
        + [jnp.zeros((4, third), jnp.float32)],
        axis=0,
    )
    row = lax.broadcasted_iota(jnp.int32, wide.shape, 0)
    head = jnp.where(row < 12, wide, 0.0)
    return jnp.concatenate([head, tail], axis=1).astype(jnp.bfloat16)


def squares_kernel(documents, squares):
    wide = documents[...].astype(jnp.float32)
    squares[...] = jnp.sum(wide * wide, axis=1, keepdims=True)


def early_kernel(place, documents, squares, *rest):
    pieces, (scores, query_squares, whole) = rest[:-3], rest[-3:]
    whole[...] = jnp.zeros_like(whole)
    for s, piece in enumerate(pieces):
        whole[pl.ds(pl.multiple_of(place[s] * 16, 16), 16), :] = unpack(piece[...])
    lane = lax.broadcasted_iota(jnp.int32, scores.shape, 1)
    raw = lax.dot_general(documents[...], whole[...], NT, preferred_element_type=jnp.float32)
    scores[...] = jnp.where(lane == 12, squares[...], raw)
    own = lax.dot_general(whole[...], whole[...], NT, preferred_element_type=jnp.float32)
    eye = lax.broadcasted_iota(jnp.int32, own.shape, 0) == lax.broadcasted_iota(jnp.int32, own.shape, 1)
    query_squares[...] = jnp.broadcast_to(
        jnp.sum(jnp.where(eye, own, 0.0), axis=0, keepdims=True), query_squares.shape
    )


def spread(narrow, place, width):
    wide = jnp.concatenate(
        [narrow, jnp.zeros((narrow.shape[0], width - narrow.shape[1]), jnp.float32)], axis=1
    )
    return pltpu.roll(wide, place * 16, 1)


def late_kernel(place, documents, piece, scores, query_squares, keep, send):
    half = keep.shape[0] - 8
    width = keep.shape[1]
    last = unpack(piece[...])
    own = lax.dot_general(last, last, NT, preferred_element_type=jnp.float32)
    eye = lax.broadcasted_iota(jnp.int32, own.shape, 0) == lax.broadcasted_iota(jnp.int32, own.shape, 1)
    own = jnp.broadcast_to(jnp.sum(jnp.where(eye, own, 0.0), axis=0, keepdims=True), (8, 16))
    row = query_squares[...] + spread(own, place[0], width)
    for to, core in ((send, 1 - place[1]), (keep, place[1])):
        rows = pl.ds(pl.multiple_of(core * half, 16), half)
        raw = lax.dot_general(documents[rows, :], last, NT, preferred_element_type=jnp.float32)
        to[:half, :] = scores[rows, :] + spread(raw, place[0], width)
        to[half:, :] = row


def finish_kernel(coordinates, keep, got, scores):
    half = scores.shape[0]
    total = keep[...] + got[...]
    doc_scale = lax.rsqrt(total[:half, 12:13] / coordinates + EPS)
    query_scale = lax.rsqrt(total[half : half + 1, :] / coordinates + EPS) / math.sqrt(coordinates)
    scaled = total[:half] * doc_scale * query_scale
    scores[...] = jnp.concatenate(
        [scaled[:, 16 * j : 16 * j + 12] for j in range(scores.shape[1] // 12)], axis=1
    )


def squared_paths(blocks):
    one = [(b, b ^ 1) for b in range(blocks)]
    two = [(b, b ^ 2) for b in range(blocks)]
    far = [(b, b ^ 4) for b in range(blocks)]
    first = [(2 * b, 2 * c) for b, c in two] + [(2 * b + 1, 2 * c + 1) for b, c in one]
    second = [(2 * b, 2 * c) for b, c in one] + [(2 * b + 1, 2 * c + 1) for b, c in two]
    return far, first, second


def by_squares(documents, queries, preconditioner):
    docs, width = documents.shape
    blocks = lax.axis_size("blk")
    half = docs // 2
    me, core = lax.axis_index("blk"), lax.axis_index("proj")
    far, first, second = squared_paths(blocks)
    packed = pl.pallas_call(
        pack_kernel,
        out_shape=jax.ShapeDtypeStruct((16, 3 * width // 4), jnp.bfloat16),
        in_specs=[vmem()] * 2,
        out_specs=vmem(),
        compiler_params=params(),
        name="pack",
    )(queries, preconditioner.reshape(1, width))
    squares = pl.pallas_call(
        squares_kernel,
        out_shape=jax.ShapeDtypeStruct((docs, 1), jnp.float32),
        in_specs=[vmem()],
        out_specs=vmem(),
        compiler_params=params(),
        name="squares",
    )(documents)
    across = lax.ppermute(packed, "blk", far)
    n1 = lax.ppermute(packed, BOTH, first)
    n2 = lax.ppermute(packed, BOTH, second)
    n3 = lax.ppermute(n1, BOTH, second)
    a1 = lax.ppermute(across, BOTH, first)
    a2 = lax.ppermute(across, BOTH, second)
    a3 = lax.ppermute(a1, BOTH, second)
    early = [packed, n1, n2, n3, across, a1, a2]
    m1, m2 = 2 - core, 1 + core
    zero = jnp.zeros_like(me)
    places = jnp.stack([me, me ^ m1, me ^ m2, me ^ 3, me ^ 4, me ^ 4 ^ m1, me ^ 4 ^ m2]).astype(jnp.int32)
    scores, query_squares = pl.pallas_call(
        early_kernel,
        out_shape=(
            jax.ShapeDtypeStruct((docs, 16 * blocks), jnp.float32),
            jax.ShapeDtypeStruct((8, 16 * blocks), jnp.float32),
        ),
        in_specs=[smem()] + [vmem()] * (2 + len(early)),
        out_specs=(vmem(), vmem()),
        scratch_shapes=[pltpu.VMEM((16 * blocks, width), jnp.bfloat16)],
        compiler_params=params(),
        name="early",
    )(places, documents, squares, *early)
    message = jax.ShapeDtypeStruct((half + 8, 16 * blocks), jnp.float32)
    keep, send = pl.pallas_call(
        late_kernel,
        out_shape=(message, message),
        in_specs=[smem()] + [vmem()] * 4,
        out_specs=(vmem(), vmem()),
        compiler_params=params(),
        name="late",
    )(jnp.stack([me ^ 7, core]).astype(jnp.int32), documents, a3, scores, query_squares)
    got = lax.ppermute(send, "proj", [(0, 1), (1, 0)])
    return pl.pallas_call(
        functools.partial(finish_kernel, 2 * width),
        out_shape=jax.ShapeDtypeStruct((half, 12 * blocks), jnp.float32),
        in_specs=[vmem()] * 2,
        out_specs=vmem(),
        compiler_params=params(),
        name="finish",
    )(keep, got)


def by_gather(documents, queries, preconditioner):
    docs, width = documents.shape
    coordinates = width * lax.axis_size("proj")
    half = docs // lax.axis_size("proj")
    weighted = (queries.astype(jnp.float32) * preconditioner[None, :]).astype(jnp.bfloat16)
    everyone = lax.all_gather(weighted, "blk", axis=0, tiled=True)
    raw = lax.dot_general(documents, everyone, NT, preferred_element_type=jnp.float32)
    doc_squares = jnp.einsum("dp,dp->d", documents, documents, preferred_element_type=jnp.float32)
    query_squares = jnp.einsum("qp,qp->q", everyone, everyone, preferred_element_type=jnp.float32)
    doc_squares, query_squares = lax.psum((doc_squares, query_squares), "proj")
    raw = lax.psum_scatter(raw, "proj", scatter_dimension=0, tiled=True)
    mine = lax.dynamic_slice_in_dim(doc_squares, lax.axis_index("proj") * half, half, 0)
    doc_scale = lax.rsqrt(mine / coordinates + EPS)
    query_scale = lax.rsqrt(query_squares / coordinates + EPS)
    return raw * doc_scale[:, None] * query_scale[None, :] / math.sqrt(coordinates)


def on_device(documents, queries, preconditioner):
    rows, width = queries.shape
    squares = lax.axis_size("blk") == 8 and lax.axis_size("proj") == 2
    if squares and rows == 12 and width % 512 == 0 and documents.shape[0] % 32 == 0:
        return by_squares(documents, queries, preconditioner)
    return by_gather(documents, queries, preconditioner)


def solution(mesh):
    placed = (P(("groups", "blk"), "proj"), P(("groups", "blk"), "proj"), P("proj"))
    return jax.shard_map(
        on_device,
        mesh=mesh,
        in_specs=placed,
        out_specs=P(("groups", "blk", "proj"), None),
        check_vma=False,
    )
```

time: 75.1 us -> 27.9 us (0.37)
  blocking collectives: 28 us -> 0 us
  between operations: 14.1 us -> 0.04 us
  waiting for transfers between devices: 16.3 us -> 7.76 us
  Pallas kernels: 0 us -> 5.72 us
  starting transfers between devices: 5.48 us -> 10.4 us
  local copies, waits for them, and re-layouts: 6.54 us -> 3.6 us
  matrix products: 2.56 us -> 0 us
  other arithmetic: 1.79 us -> 0.07 us
    unnamed x1 -> x0, blocking collectives: 23.1 us -> none
    all_gather x1 -> x0, waiting for transfers between devices: 16 us -> none  [on_device(): lax.all_gather(widened, 'blk', axis=0, tiled=True)]
    ppermute x0 -> x8, starting transfers between devices: none -> 10.4 us  [the longest x1 4.1 us: by_squares(): across = lax.ppermute(packed, 'blk', far)]
    ppermute x0 -> x8, waiting for transfers between devices: none -> 7.76 us  [the longest x1 3.43 us: by_squares(): across = lax.ppermute(packed, 'blk', far)]
    pallas_call x0 -> x5, Pallas kernels: none -> 5.72 us  [the longest x1 2.4 us: by_squares(): pl.pallas_call(early_kernel, out_shape=(jax.ShapeDtypeStruct((docs, 16 *...]
    all_to_all x1 -> x0, starting transfers between devices: 5.48 us -> none  [on_device(): lax.all_to_all(documents, 'proj', split_axis=0, concat_axis=1, tiled=True)]
    psum x1 -> x0, blocking collectives: 2.7 us -> none  [on_device(): doc_squares, query_squares = lax.psum((doc_squares, query_squares), 'proj')]
    dot_general x1 -> x0, matrix products: 2.56 us -> none  [make_folder(): lax.dot_general(doc_block, query_piece, (((1,), (1,)), ((), ())), preferr...]
  transfers between devices with their start and end apart: 2 -> 8, of which waited for: 2 -> 4; matrix products, arithmetic and copies ran while one was open for 5% -> 1% of each run, Pallas kernels for 0% -> 11%
where the time goes in v1:
time: 27.9 us; the launch traced here: 27.6 us
  starting transfers between devices  10.4 us (37%)
  waiting for transfers between devices  7.76 us (28%)
  Pallas kernels  5.72 us (21%)
  local copies, waits for them, and re-layouts  3.6 us (13%)
    ppermute x1, starting transfers between devices, by_squares(): across = lax.ppermute(packed, 'blk', far)  4.1 us
    unnamed x8, local copies, waits for them, and re-layouts  3.51 us
    ppermute x1, waiting for transfers between devices, by_squares(): across = lax.ppermute(packed, 'blk', far)  3.43 us
    pallas_call x1, Pallas kernels, by_squares(): pl.pallas_call(early_kernel, out_shape=(jax.ShapeDtypeStruct((docs, 16 *...  2.4 us
    ppermute x1, waiting for transfers between devices, by_squares(): a2 = lax.ppermute(across, BOTH, second)  1.97 us
    pallas_call x1, Pallas kernels, by_squares(): pl.pallas_call(late_kernel, out_shape=(message, message), in_specs=[smem(...  1.62 us
    ppermute x1, starting transfers between devices, by_squares(): n1 = lax.ppermute(packed, BOTH, first)  1.58 us
    ppermute x1, starting transfers between devices, by_squares(): n3 = lax.ppermute(n1, BOTH, second)  1.49 us
  transfers between devices with their start and end apart: 8, of which 4 were waited for; matrix products, arithmetic and copies ran while one was open for 1% of the time, Pallas kernels for 11%

profile of v1, /device:TPU:0, one launch (start us, length us, event | category | flops | bytes accessed | tf_op | source)
XLA Modules:
  0.0 27.6 jit_solution(16520860677507854637)
XLA Ops:
  0.0 0.9 %copy-done.2 = bf16[12,4096]{1,0:T(8,128)(2,1)S(1)} copy-done((bf16[12,4096]{1,0:T(8,128)(2,1)S(1)}, bf16[12,4096]{1,0:T(8,128)(2,1)}, u32[]{:S(2)}) %copy-start.2) | copy-done | bytes 98328
  0.9 0.7 %copy-done.3 = f32[4096]{0:T(1024)S(1)} copy-done((f32[4096]{0:T(1024)S(1)}, f32[4096]{0:T(1024)}, u32[]{:S(2)}) %copy-start.3) | copy-done | bytes 16408
  1.7 4.1 %collective-permute-start = (bf16[16,3072]{1,0:T(8,128)(2,1)S(1)}, bf16[16,3072]{1,0:T(8,128)(2,1)S(1)}, u32[]{:S(2)}, u32[]{:S(2)}) collective-permute-start(bf16[16,3072]{1,0:T(8,128)(2,1)S(1)} %pack.1.rest_0_), channel_id=1, source_target_pairs={{0,8},{2,10},{4,12},{6,14},{8,0},{10,2},{12,4},{14,6},{1,9},{3,11}... | collective-permute-start | bytes 294920 | tf_op jit(solution)/shard_map/ppermute | solution.py:135
  5.8 1.6 %collective-permute-start.3 = (bf16[16,3072]{1,0:T(8,128)(2,1)S(1)}, bf16[16,3072]{1,0:T(8,128)(2,1)}, u32[]{:S(2)}, u32[]{:S(2)}) collective-permute-start(bf16[16,3072]{1,0:T(8,128)(2,1)S(1)} %pack.1.rest_0_), channel_id=1, source_target_pairs={{0,4},{2,6},{4,0},{6,2},{8,12},{10,14},{12,8},{14,10},{1,3},{3,1},... | collective-permute-start | bytes 294920 | tf_op jit(solution)/shard_map/ppermute | solution.py:136
  7.3 3.4 %collective-permute-done.rest_4_ = bf16[16,3072]{1,0:T(8,128)(2,1)S(1)} collective-permute-done((bf16[16,3072]{1,0:T(8,128)(2,1)S(1)}, bf16[16,3072]{1,0:T(8,128)(2,1)S(1)}, u32[]{:S(2)}, u32[]{:S(2)}) %collective-permute-start) | collective-permute-done | bytes 98336 | tf_op jit(solution)/shard_map/ppermute | solution.py:135
  10.8 0.6 %collective-permute-start.1 = (bf16[16,3072]{1,0:T(8,128)(2,1)S(1)}, bf16[16,3072]{1,0:T(8,128)(2,1)}, u32[]{:S(2)}, u32[]{:S(2)}) collective-permute-start(bf16[16,3072]{1,0:T(8,128)(2,1)S(1)} %collective-permute-done.rest_4_), channel_id=1, source_target_pairs={{0,4},{2,6},{4,0},{6,2},{8,12},{10,14},{12,8},{14,10},{1,3},{3,1},... | collective-permute-start | bytes 294920 | tf_op jit(solution)/shard_map/ppermute | solution.py:139
  11.4 1.5 %collective-permute-start.4 = (bf16[16,3072]{1,0:T(8,128)(2,1)S(1)}, bf16[16,3072]{1,0:T(8,128)(2,1)}, u32[]{:S(2)}, u32[]{:S(2)}) collective-permute-start(bf16[16,3072]{1,0:T(8,128)(2,1)S(1)} %pack.1.rest_0_), channel_id=1, source_target_pairs={{0,2},{2,0},{4,6},{6,4},{8,10},{10,8},{12,14},{14,12},{1,5},{3,7},... | collective-permute-start | bytes 294920 | tf_op jit(solution)/shard_map/ppermute | solution.py:137
  12.9 1.9 %copy-done = bf16[384,4096]{1,0:T(8,128)(2,1)S(1)} copy-done((bf16[384,4096]{1,0:T(8,128)(2,1)S(1)}, bf16[384,4096]{1,0:T(8,128)(2,1)}, u32[]{:S(2)}) %copy-start) | copy-done | bytes 3145752
  14.8 0.7 %squares.1 = f32[384,1]{1,0:T(8,128)S(1)} custom-call(bf16[384,4096]{1,0:T(8,128)(2,1)S(1)} %copy-done), custom_call_target="tpu_custom_call" | custom-call | tf_op jit(solution)/shard_map/squares/pallas_call | solution.py:127
  15.5 0.1 stack.43.place
  15.5 0.5 %collective-permute-start.6 = (bf16[16,3072]{1,0:T(8,128)(2,1)S(1)}, bf16[16,3072]{1,0:T(8,128)(2,1)S(1)}, u32[]{:S(2)}, u32[]{:S(2)}) collective-permute-start(bf16[16,3072]{1,0:T(8,128)(2,1)S(1)} %collective-permute-done.rest_4_), channel_id=1, source_target_pairs={{0,2},{2,0},{4,6},{6,4},{8,10},{10,8},{12,14},{14,12},{1,5},{3,7},... | collective-permute-start | bytes 294920 | tf_op jit(solution)/shard_map/ppermute | solution.py:140
  16.1 0.0 collective-permute-done.3.rest_1_
  16.1 1.5 %collective-permute-start.5 = (bf16[16,3072]{1,0:T(8,128)(2,1)}, bf16[16,3072]{1,0:T(8,128)(2,1)S(1)}, u32[]{:S(2)}, u32[]{:S(2)}) collective-permute-start(bf16[16,3072]{1,0:T(8,128)(2,1)} %collective-permute-done.3.rest_1_), channel_id=1, source_target_pairs={{0,2},{2,0},{4,6},{6,4},{8,10},{10,8},{12,14},{14,12},{1,5},{3,7},... | collective-permute-start | bytes 294920 | tf_op jit(solution)/shard_map/ppermute | solution.py:138
  17.6 0.0 collective-permute-done.1.rest_5_
  17.6 0.5 %collective-permute-start.2 = (bf16[16,3072]{1,0:T(8,128)(2,1)}, bf16[16,3072]{1,0:T(8,128)(2,1)S(1)}, u32[]{:S(2)}, u32[]{:S(2)}) collective-permute-start(bf16[16,3072]{1,0:T(8,128)(2,1)} %collective-permute-done.1.rest_5_), channel_id=1, source_target_pairs={{0,2},{2,0},{4,6},{6,4},{8,10},{10,8},{12,14},{14,12},{1,5},{3,7},... | collective-permute-start | bytes 294920 | tf_op jit(solution)/shard_map/ppermute | solution.py:141
  18.1 0.1 pad_add_fusion.place
  18.2 2.0 %collective-permute-done.6.rest_6_ = bf16[16,3072]{1,0:T(8,128)(2,1)S(1)} collective-permute-done((bf16[16,3072]{1,0:T(8,128)(2,1)S(1)}, bf16[16,3072]{1,0:T(8,128)(2,1)S(1)}, u32[]{:S(2)}, u32[]{:S(2)}) %collective-permute-start.6) | collective-permute-done | bytes 98336 | tf_op jit(solution)/shard_map/ppermute | solution.py:140
  20.2 1.1 %collective-permute-done.5.rest_3_ = bf16[16,3072]{1,0:T(8,128)(2,1)S(1)} collective-permute-done((bf16[16,3072]{1,0:T(8,128)(2,1)}, bf16[16,3072]{1,0:T(8,128)(2,1)S(1)}, u32[]{:S(2)}, u32[]{:S(2)}) %collective-permute-start.5) | collective-permute-done | bytes 98336 | tf_op jit(solution)/shard_map/ppermute | solution.py:138
  21.2 2.4 %early.1 = (f32[384,128]{1,0:T(8,128)S(1)}, f32[8,128]{1,0:T(8,128)S(1)}) custom-call(s32[7]{0:T(128)S(1)} %stack.43.place, bf16[384,4096]{1,0:T(8,128)(2,1)S(1)} %copy-done.1, f32[384,1]{1,0:T(8,128)S(1)} %squares.1, bf16[16,3072]{1,0:T(8,128)(2,1)S(1)} %pack.1.rest_0_, bf16[16,3072]{1,0:T(8,128)(2,1)} %collective-permute-done.3.rest_1_, ...), custom_call_target="tpu_custom_call" | custom-call | tf_op jit(solution)/shard_map/early/pallas_call | solution.py:146
  23.6 0.0 collective-permute-done.2.piece
  23.6 1.6 %late.1 = (f32[200,128]{1,0:T(8,128)S(1)}, f32[200,128]{1,0:T(8,128)S(1)}) custom-call(s32[2]{0:T(128)S(1)} %pad_add_fusion.place, bf16[384,4096]{1,0:T(8,128)(2,1)S(1)} %copy-done.1, bf16[16,3072]{1,0:T(8,128)(2,1)S(1)} %collective-permute-done.2.piece, f32[384,128]{1,0:T(8,128)S(1)} %get-tuple-element.9.scores, f32[8,128]{1,0:T(8,128)S(1)} %get-tuple-element.10.query_squares), custom_call_target="tpu_custom_call" | custom-call | tf_op jit(solution)/shard_map/late/pallas_call | solution.py:159
  25.3 0.1 collective-permute-start.7
  25.3 1.3 %collective-permute-done.7.got = f32[200,128]{1,0:T(8,128)S(1)} collective-permute-done((f32[200,128]{1,0:T(8,128)S(1)}, f32[200,128]{1,0:T(8,128)S(1)}, u32[]{:S(2)}, u32[]{:S(2)}) %collective-permute-start.7) | collective-permute-done | bytes 102432 | tf_op jit(solution)/shard_map/ppermute | solution.py:167
  26.6 1.0 %finish.1 = f32[192,96]{1,0:T(8,128)} custom-call(f32[200,128]{1,0:T(8,128)S(1)} %get-tuple-element.11.keep, f32[200,128]{1,0:T(8,128)S(1)} %collective-permute-done.7.got), custom_call_target="tpu_custom_call" | custom-call | tf_op jit(solution)/shard_map/finish/pallas_call | solution.py:168
  (7 shorter events, 0.0 us)
Async XLA Ops:
  0.0 0.9 %copy-start.2 = (bf16[12,4096]{1,0:T(8,128)(2,1)S(1)}, bf16[12,4096]{1,0:T(8,128)(2,1)}, u32[]{:S(2)}) copy-start(bf16[12,4096]{1,0:T(8,128)(2,1)} %queries.1) | copy-start | bytes 294916
  0.9 0.7 %copy-start.3 = (f32[4096]{0:T(1024)S(1)}, f32[4096]{0:T(1024)}, u32[]{:S(2)}) copy-start(f32[4096]{0:T(1024)} %param.5) | copy-start | bytes 49156
  1.7 9.1 %collective-permute-start = (bf16[16,3072]{1,0:T(8,128)(2,1)S(1)}, bf16[16,3072]{1,0:T(8,128)(2,1)S(1)}, u32[]{:S(2)}, u32[]{:S(2)}) collective-permute-start(bf16[16,3072]{1,0:T(8,128)(2,1)S(1)} %pack.1.rest_0_), channel_id=1, source_target_pairs={{0,8},{2,10},{4,12},{6,14},{8,0},{10,2},{12,4},{14,6},{1,9},{3,11}... | collective-permute-start | bytes 294920 | tf_op jit(solution)/shard_map/ppermute | solution.py:135
  5.8 10.3 %collective-permute-start.3 = (bf16[16,3072]{1,0:T(8,128)(2,1)S(1)}, bf16[16,3072]{1,0:T(8,128)(2,1)}, u32[]{:S(2)}, u32[]{:S(2)}) collective-permute-start(bf16[16,3072]{1,0:T(8,128)(2,1)S(1)} %pack.1.rest_0_), channel_id=1, source_target_pairs={{0,4},{2,6},{4,0},{6,2},{8,12},{10,14},{12,8},{14,10},{1,3},{3,1},... | collective-permute-start | bytes 294920 | tf_op jit(solution)/shard_map/ppermute | solution.py:136
  10.8 6.8 %collective-permute-start.1 = (bf16[16,3072]{1,0:T(8,128)(2,1)S(1)}, bf16[16,3072]{1,0:T(8,128)(2,1)}, u32[]{:S(2)}, u32[]{:S(2)}) collective-permute-start(bf16[16,3072]{1,0:T(8,128)(2,1)S(1)} %collective-permute-done.rest_4_), channel_id=1, source_target_pairs={{0,4},{2,6},{4,0},{6,2},{8,12},{10,14},{12,8},{14,10},{1,3},{3,1},... | collective-permute-start | bytes 294920 | tf_op jit(solution)/shard_map/ppermute | solution.py:139
  11.4 6.8 %collective-permute-start.4 = (bf16[16,3072]{1,0:T(8,128)(2,1)S(1)}, bf16[16,3072]{1,0:T(8,128)(2,1)}, u32[]{:S(2)}, u32[]{:S(2)}) collective-permute-start(bf16[16,3072]{1,0:T(8,128)(2,1)S(1)} %pack.1.rest_0_), channel_id=1, source_target_pairs={{0,2},{2,0},{4,6},{6,4},{8,10},{10,8},{12,14},{14,12},{1,5},{3,7},... | collective-permute-start | bytes 294920 | tf_op jit(solution)/shard_map/ppermute | solution.py:137
  12.9 1.9 %copy-start = (bf16[384,4096]{1,0:T(8,128)(2,1)S(1)}, bf16[384,4096]{1,0:T(8,128)(2,1)}, u32[]{:S(2)}) copy-start(bf16[384,4096]{1,0:T(8,128)(2,1)} %documents.5) | copy-start | bytes 9437188
  14.8 6.5 %copy-start.1 = (bf16[384,4096]{1,0:T(8,128)(2,1)S(1)}, bf16[384,4096]{1,0:T(8,128)(2,1)}, u32[]{:S(2)}) copy-start(bf16[384,4096]{1,0:T(8,128)(2,1)} %documents.5) | copy-start | bytes 9437188
  15.5 4.6 %collective-permute-start.6 = (bf16[16,3072]{1,0:T(8,128)(2,1)S(1)}, bf16[16,3072]{1,0:T(8,128)(2,1)S(1)}, u32[]{:S(2)}, u32[]{:S(2)}) collective-permute-start(bf16[16,3072]{1,0:T(8,128)(2,1)S(1)} %collective-permute-done.rest_4_), channel_id=1, source_target_pairs={{0,2},{2,0},{4,6},{6,4},{8,10},{10,8},{12,14},{14,12},{1,5},{3,7},... | collective-permute-start | bytes 294920 | tf_op jit(solution)/shard_map/ppermute | solution.py:140
  16.1 5.1 %collective-permute-start.5 = (bf16[16,3072]{1,0:T(8,128)(2,1)}, bf16[16,3072]{1,0:T(8,128)(2,1)S(1)}, u32[]{:S(2)}, u32[]{:S(2)}) collective-permute-start(bf16[16,3072]{1,0:T(8,128)(2,1)} %collective-permute-done.3.rest_1_), channel_id=1, source_target_pairs={{0,2},{2,0},{4,6},{6,4},{8,10},{10,8},{12,14},{14,12},{1,5},{3,7},... | collective-permute-start | bytes 294920 | tf_op jit(solution)/shard_map/ppermute | solution.py:138
  17.6 6.0 %collective-permute-start.2 = (bf16[16,3072]{1,0:T(8,128)(2,1)}, bf16[16,3072]{1,0:T(8,128)(2,1)S(1)}, u32[]{:S(2)}, u32[]{:S(2)}) collective-permute-start(bf16[16,3072]{1,0:T(8,128)(2,1)} %collective-permute-done.1.rest_5_), channel_id=1, source_target_pairs={{0,2},{2,0},{4,6},{6,4},{8,10},{10,8},{12,14},{14,12},{1,5},{3,7},... | collective-permute-start | bytes 294920 | tf_op jit(solution)/shard_map/ppermute | solution.py:141
  25.3 1.4 %collective-permute-start.7 = (f32[200,128]{1,0:T(8,128)S(1)}, f32[200,128]{1,0:T(8,128)S(1)}, u32[]{:S(2)}, u32[]{:S(2)}) collective-permute-start(f32[200,128]{1,0:T(8,128)S(1)} %get-tuple-element.12), channel_id=1, source_target_pairs={{0,1},{1,0},{2,3},{3,2},{4,5},{5,4},{6,7},{7,6},{8,9},{9,8},{10,11... | collective-permute-start | bytes 307208 | tf_op jit(solution)/shard_map/ppermute | solution.py:167

commit v2 on v0

v2 whole, which is shorter than its diff:
```python
import functools
import math

import jax
import jax.numpy as jnp
from jax import lax
from jax.experimental import pallas as pl
from jax.experimental.pallas import tpu as pltpu
from jax.sharding import PartitionSpec as P

EPS = 1e-06
MIB = 1024 * 1024
BOTH = ("blk", "proj")
NT = (((1,), (1,)), ((), ()))


def vmem():
    return pl.BlockSpec(memory_space=pltpu.VMEM)


def smem():
    return pl.BlockSpec(memory_space=pltpu.SMEM)


def anywhere():
    return pl.BlockSpec(memory_space=pl.ANY)


def pack_kernel(queries_hbm, preconditioner_hbm, packed, queries, preconditioner, arrived):
    copies = [
        pltpu.make_async_copy(queries_hbm, queries, arrived.at[0]),
        pltpu.make_async_copy(preconditioner_hbm, preconditioner, arrived.at[1]),
    ]
    for copy in copies:
        copy.start()
    for copy in copies:
        copy.wait()
    width = queries.shape[1]
    weighted = queries[...].astype(jnp.float32) * preconditioner[...]
    packed[:, :width] = weighted[:8].astype(packed.dtype)
    tail = jnp.concatenate([weighted[8:, : width // 2], weighted[8:, width // 2 :]], axis=0)
    packed[:, width:] = tail.astype(packed.dtype)


def join_kernel(first, second, joined):
    rows = first.shape[0]
    joined[:rows] = first[...]
    joined[rows:] = second[...]


def squares_kernel(documents, squares):
    wide = documents[...].astype(jnp.float32)
    squares[...] = jnp.sum(wide * wide, axis=1, keepdims=True)


def blocks_from(steps):
    me, core = lax.axis_index("blk"), lax.axis_index("proj")
    return [me ^ (step if isinstance(step, int) else step[0] + (step[1] - step[0]) * core) for step in steps]


def unpack(packed):
    width = 2 * packed.shape[1] // 3
    tail = packed[:, width:]
    return jnp.concatenate([packed[:, :width], jnp.concatenate([tail, tail], axis=1)], axis=0)


def scatter(places, pieces, whole):
    whole[...] = jnp.zeros_like(whole)
    for place, piece in zip(places, pieces):
        whole[pl.ds(pl.multiple_of(place * 16, 16), 16), :] = unpack(piece)


def products(left, whole):
    middle = whole.shape[1] // 2
    low = lax.dot_general(left[:, :middle], whole[:, :middle], NT, preferred_element_type=jnp.float32)
    high = lax.dot_general(left[:, middle:], whole[:, middle:], NT, preferred_element_type=jnp.float32)
    lane = lax.broadcasted_iota(jnp.int32, low.shape, 1) & 15
    moved = pltpu.roll(high, low.shape[1] - 4, 1)
    return jnp.where(lane < 8, low + high, jnp.where(lane < 12, low + moved, 0.0))


def own_squares(places, pieces, lanes):
    lane = lax.broadcasted_iota(jnp.int32, (8, lanes), 1)
    row = lax.broadcasted_iota(jnp.int32, (8, lanes), 0)
    total = jnp.zeros((8, lanes), jnp.float32)
    for place, piece in zip(places, pieces):
        width = 2 * piece.shape[1] // 3
        wide = piece.astype(jnp.float32)
        wide = wide * wide
        head = jnp.sum(wide[:, :width], axis=1, keepdims=True)
        tail = jnp.sum(wide[:, width:], axis=1, keepdims=True)
        total += jnp.where(lane == place * 16 + row, head, 0.0)
        total += jnp.where(lane == place * 16 + 8 + (row & 3), tail, 0.0)
    return jnp.broadcast_to(jnp.sum(total, axis=0, keepdims=True), (8, lanes))


def early_kernel(steps, documents, squares, *rest):
    refs, (scores, query_squares, whole) = rest[:-3], rest[-3:]
    places, pieces = blocks_from(steps), [ref[r : r + 8] for ref in refs for r in range(0, ref.shape[0], 8)]
    scatter(places, pieces, whole)
    lane = lax.broadcasted_iota(jnp.int32, scores.shape, 1)
    scores[...] = jnp.where(lane == 12, squares[...], products(documents, whole))
    query_squares[...] = own_squares(places, pieces, scores.shape[1])


def late_kernel(steps, other, documents, *rest):
    refs, (scores, query_squares, out, whole) = rest[:-4], rest[-4:]
    half = out.shape[0] - 8
    places, pieces = blocks_from(steps), [ref[r : r + 8] for ref in refs for r in range(0, ref.shape[0], 8)]
    scatter(places, pieces, whole)
    core = lax.axis_index("proj")
    side = 1 - core if other else core
    rows = pl.ds(pl.multiple_of(side * half, 16), half)
    out[:half, :] = scores[rows, :] + products(documents.at[rows], whole)
    out[half:, :] = query_squares[...] + own_squares(places, pieces, out.shape[1])


def finish_kernel(coordinates, keep, got, scores):
    half = scores.shape[0]
    total = keep[...] + got[...]
    doc_scale = lax.rsqrt(total[:half, 12:13] / coordinates + EPS)
    query_scale = lax.rsqrt(total[half : half + 1, :] / coordinates + EPS) / math.sqrt(coordinates)
    scaled = total[:half] * doc_scale * query_scale
    scores[...] = jnp.concatenate(
        [scaled[:, 16 * j : 16 * j + 12] for j in range(scores.shape[1] // 12)], axis=1
    )


def squared_paths(blocks):
    one = [(b, b ^ 1) for b in range(blocks)]
    two = [(b, b ^ 2) for b in range(blocks)]
    far = [(b, b ^ 4) for b in range(blocks)]
    first = [(2 * b, 2 * c) for b, c in two] + [(2 * b + 1, 2 * c + 1) for b, c in one]
    second = [(2 * b, 2 * c) for b, c in one] + [(2 * b + 1, 2 * c + 1) for b, c in two]
    farthest = [(b, b ^ 7) for b in range(blocks)]
    return far, farthest, first, second


def call(kernel, name, out, *args, hbm=False, scratch=(), limit=24):
    return pl.pallas_call(
        kernel,
        out_shape=out,
        in_specs=[anywhere() if hbm else vmem()] * len(args),
        out_specs=jax.tree.map(lambda _: vmem(), out),
        scratch_shapes=scratch,
        compiler_params=pltpu.CompilerParams(vmem_limit_bytes=limit * MIB),
        name=name,
        cost_estimate=pl.CostEstimate(flops=int({"early":2e10,"squares":2e10}.get(name, 1e9)), bytes_accessed=4194304, transcendentals=0),
    )(*args)


def by_squares(documents, queries, preconditioner):
    docs, width = documents.shape
    blocks = lax.axis_size("blk")
    half = docs // 2
    lanes = 16 * blocks
    far, farthest, first, second = squared_paths(blocks)
    packed = call(
        pack_kernel,
        "pack",
        pltpu.VMEM((8, 3 * width // 2), jnp.bfloat16),
        queries,
        preconditioner.reshape(1, width),
        hbm=True,
        limit=24,
        scratch=[
            pltpu.VMEM(queries.shape, queries.dtype),
            pltpu.VMEM((1, width), jnp.float32),
            pltpu.SemaphoreType.DMA((2,)),
        ],
    )
    across = lax.ppermute(packed, "blk", far)
    n1 = lax.ppermute(packed, BOTH, first)
    n2 = lax.ppermute(packed, BOTH, second)
    corner = lax.ppermute(packed, "blk", farthest)
    squares = call(squares_kernel, "squares", pltpu.VMEM((docs, 1), jnp.float32), documents)
    across, n1, n2, squares = lax.optimization_barrier((across, n1, n2, squares))
    a1 = lax.ppermute(across, BOTH, first)
    two = call(join_kernel, "join", pltpu.VMEM((16, 3 * width // 2), jnp.bfloat16), n1, across)
    pair = lax.ppermute(two, BOTH, second)
    whole = pltpu.VMEM((lanes, width), jnp.bfloat16)
    scores, query_squares = call(
        functools.partial(early_kernel, (0, (1, 2), (2, 1), 4)),
        "early",
        (pltpu.VMEM((docs, lanes), jnp.float32), pltpu.VMEM((8, lanes), jnp.float32)),
        documents,
        squares,
        packed,
        n2,
        two,
        scratch=[whole],
    )
    send, keep = (
        call(
            functools.partial(late_kernel, (7, (6, 5), 3, (5, 6)), other),
            "late",
            pltpu.VMEM((half + 8, lanes), jnp.float32),
            documents,
            corner,
            a1,
            pair,
            scores,
            query_squares,
            scratch=[whole],
        )
        for other in (True, False)
    )
    got = lax.ppermute(send, "proj", [(0, 1), (1, 0)])
    return call(
        functools.partial(finish_kernel, 2 * width),
        "finish",
        jax.ShapeDtypeStruct((half, 12 * blocks), jnp.float32),
        keep,
        got,
    )


def by_gather(documents, queries, preconditioner):
    docs, width = documents.shape
    coordinates = width * lax.axis_size("proj")
    half = docs // lax.axis_size("proj")
    weighted = (queries.astype(jnp.float32) * preconditioner[None, :]).astype(jnp.bfloat16)
    everyone = lax.all_gather(weighted, "blk", axis=0, tiled=True)
    raw = lax.dot_general(documents, everyone, NT, preferred_element_type=jnp.float32)
    doc_squares = jnp.einsum("dp,dp->d", documents, documents, preferred_element_type=jnp.float32)
    query_squares = jnp.einsum("qp,qp->q", everyone, everyone, preferred_element_type=jnp.float32)
    doc_squares, query_squares = lax.psum((doc_squares, query_squares), "proj")
    raw = lax.psum_scatter(raw, "proj", scatter_dimension=0, tiled=True)
    mine = lax.dynamic_slice_in_dim(doc_squares, lax.axis_index("proj") * half, half, 0)
    doc_scale = lax.rsqrt(mine / coordinates + EPS)
    query_scale = lax.rsqrt(query_squares / coordinates + EPS)
    return raw * doc_scale[:, None] * query_scale[None, :] / math.sqrt(coordinates)


def on_device(documents, queries, preconditioner):
    rows, width = queries.shape
    squares = lax.axis_size("blk") == 8 and lax.axis_size("proj") == 2
    if squares and rows == 12 and width % 512 == 0 and documents.shape[0] % 32 == 0:
        return by_squares(documents, queries, preconditioner)
    return by_gather(documents, queries, preconditioner)


def solution(mesh):
    placed = (P(("groups", "blk"), "proj"), P(("groups", "blk"), "proj"), P("proj"))
    return jax.shard_map(
        on_device,
        mesh=mesh,
        in_specs=placed,
        out_specs=P(("groups", "blk", "proj"), None),
        check_vma=False,
    )
```

time: 75.1 us -> 22.9 us (0.30)
  blocking collectives: 28 us -> 0 us
  between operations: 14.1 us -> 0.05 us
  waiting for transfers between devices: 16.3 us -> 6.17 us
  local copies, waits for them, and re-layouts: 6.54 us -> 1.77 us
  Pallas kernels: 0 us -> 4.65 us
  starting transfers between devices: 5.48 us -> 10 us
  matrix products: 2.56 us -> 0 us
  other arithmetic: 1.79 us -> 0 us
    unnamed x1 -> x0, blocking collectives: 23.1 us -> none
    all_gather x1 -> x0, waiting for transfers between devices: 16 us -> none  [on_device(): lax.all_gather(widened, 'blk', axis=0, tiled=True)]
    ppermute x0 -> x7, starting transfers between devices: none -> 10 us  [the longest x1 4.1 us: by_squares(): across = lax.ppermute(packed, 'blk', far)]
    ppermute x0 -> x7, waiting for transfers between devices: none -> 6.17 us  [the longest x1 1.45 us: by_squares(): pair = lax.ppermute(two, BOTH, second)]
    all_to_all x1 -> x0, starting transfers between devices: 5.48 us -> none  [on_device(): lax.all_to_all(documents, 'proj', split_axis=0, concat_axis=1, tiled=True)]
    pallas_call x0 -> x7, Pallas kernels: none -> 4.65 us  [call(): pl.pallas_call(kernel, out_shape=out, in_specs=[anywhere() if hbm else vm...]
    psum x1 -> x0, blocking collectives: 2.7 us -> none  [on_device(): doc_squares, query_squares = lax.psum((doc_squares, query_squares), 'proj')]
    dot_general x1 -> x0, matrix products: 2.56 us -> none  [make_folder(): lax.dot_general(doc_block, query_piece, (((1,), (1,)), ((), ())), preferr...]
  transfers between devices with their start and end apart: 2 -> 7, of which waited for: 2 -> 6; matrix products, arithmetic and copies ran while one was open for 5% -> 0% of each run, Pallas kernels for 0% -> 12%
where the time goes in v2:
time: 22.9 us; the launch traced here: 22.7 us
  starting transfers between devices  10 us (44%)
  waiting for transfers between devices  6.17 us (27%)
  Pallas kernels  4.65 us (20%)
  local copies, waits for them, and re-layouts  1.77 us (8%)
    pallas_call x7, Pallas kernels, call(): pl.pallas_call(kernel, out_shape=out, in_specs=[anywhere() if hbm else vm...  4.65 us
    ppermute x1, starting transfers between devices, by_squares(): across = lax.ppermute(packed, 'blk', far)  4.1 us
    unnamed x6, local copies, waits for them, and re-layouts  1.77 us
    ppermute x1, starting transfers between devices, by_squares(): n1 = lax.ppermute(packed, BOTH, first)  1.58 us
    ppermute x1, starting transfers between devices, by_squares(): n2 = lax.ppermute(packed, BOTH, second)  1.49 us
    ppermute x1, waiting for transfers between devices, by_squares(): pair = lax.ppermute(two, BOTH, second)  1.45 us
    ppermute x1, waiting for transfers between devices, by_squares(): a1 = lax.ppermute(across, BOTH, first)  1.43 us
    ppermute x1, starting transfers between devices, by_squares(): pair = lax.ppermute(two, BOTH, second)  1.42 us
  transfers between devices with their start and end apart: 7, of which 6 were waited for; matrix products, arithmetic and copies ran while one was open for 0% of the time, Pallas kernels for 12%

profile of v2, /device:TPU:0, one launch (start us, length us, event | category | flops | bytes accessed | tf_op | source)
XLA Modules:
  0.0 22.7 jit_solution(2846658883751693658)
XLA Ops:
  0.0 0.0 copy-start
  0.0 1.1 %copy-done.1 = bf16[12,4096]{1,0:T(8,128)(2,1)S(1)} copy-done((bf16[12,4096]{1,0:T(8,128)(2,1)S(1)}, bf16[12,4096]{1,0:T(8,128)(2,1)}, u32[]{:S(2)}) %copy-start.1) | copy-done | bytes 98328
  1.1 0.7 %copy-done.2 = f32[4096]{0:T(1024)S(1)} copy-done((f32[4096]{0:T(1024)S(1)}, f32[4096]{0:T(1024)}, u32[]{:S(2)}) %copy-start.2) | copy-done | bytes 16408
  1.8 0.2 pack.1.rest_0_
  2.0 4.1 %collective-permute-start.1 = (bf16[8,6144]{1,0:T(8,128)(2,1)S(1)}, bf16[8,6144]{1,0:T(8,128)(2,1)S(1)}, u32[]{:S(2)}, u32[]{:S(2)}) collective-permute-start(bf16[8,6144]{1,0:T(8,128)(2,1)S(1)} %pack.1.rest_0_), channel_id=1, source_target_pairs={{0,8},{2,10},{4,12},{6,14},{8,0},{10,2},{12,4},{14,6},{1,9},{3,11}... | collective-permute-start | bytes 294920 | tf_op jit(solution)/shard_map/ppermute | solution.py:172
  6.1 1.6 %collective-permute-start.2 = (bf16[8,6144]{1,0:T(8,128)(2,1)S(1)}, bf16[8,6144]{1,0:T(8,128)(2,1)S(1)}, u32[]{:S(2)}, u32[]{:S(2)}) collective-permute-start(bf16[8,6144]{1,0:T(8,128)(2,1)S(1)} %pack.1.rest_0_), channel_id=1, source_target_pairs={{0,4},{2,6},{4,0},{6,2},{8,12},{10,14},{12,8},{14,10},{1,3},{3,1},... | collective-permute-start | bytes 294920 | tf_op jit(solution)/shard_map/ppermute | solution.py:173
  7.7 1.5 %collective-permute-start.3 = (bf16[8,6144]{1,0:T(8,128)(2,1)S(1)}, bf16[8,6144]{1,0:T(8,128)(2,1)S(1)}, u32[]{:S(2)}, u32[]{:S(2)}) collective-permute-start(bf16[8,6144]{1,0:T(8,128)(2,1)S(1)} %pack.1.rest_0_), channel_id=1, source_target_pairs={{0,2},{2,0},{4,6},{6,4},{8,10},{10,8},{12,14},{14,12},{1,5},{3,7},... | collective-permute-start | bytes 294920 | tf_op jit(solution)/shard_map/ppermute | solution.py:174
  9.2 0.0 collective-permute-start
  9.2 0.0 copy-done
  9.2 0.7 %squares.1 = f32[384,1]{1,0:T(8,128)S(1)} custom-call(bf16[384,4096]{1,0:T(8,128)(2,1)S(1)} %copy-done), custom_call_target="tpu_custom_call" | custom-call | flops 20000000000 | bytes 4194304 | tf_op jit(solution)/shard_map/squares/pallas_call | solution.py:140
  9.9 1.3 %collective-permute-done.1.second = bf16[8,6144]{1,0:T(8,128)(2,1)S(1)} collective-permute-done((bf16[8,6144]{1,0:T(8,128)(2,1)S(1)}, bf16[8,6144]{1,0:T(8,128)(2,1)S(1)}, u32[]{:S(2)}, u32[]{:S(2)}) %collective-permute-start.1) | collective-permute-done | bytes 98336 | tf_op jit(solution)/shard_map/ppermute | solution.py:172
  11.2 1.2 %collective-permute-done.2.first = bf16[8,6144]{1,0:T(8,128)(2,1)S(1)} collective-permute-done((bf16[8,6144]{1,0:T(8,128)(2,1)S(1)}, bf16[8,6144]{1,0:T(8,128)(2,1)S(1)}, u32[]{:S(2)}, u32[]{:S(2)}) %collective-permute-start.2) | collective-permute-done | bytes 98336 | tf_op jit(solution)/shard_map/ppermute | solution.py:173
  12.4 0.0 collective-permute-done.3.rest_1_
  12.4 1.4 %collective-permute-start.4 = (bf16[8,6144]{1,0:T(8,128)(2,1)S(1)}, bf16[8,6144]{1,0:T(8,128)(2,1)S(1)}, u32[]{:S(2)}, u32[]{:S(2)}) collective-permute-start(bf16[8,6144]{1,0:T(8,128)(2,1)S(1)} %collective-permute-done.1.second), channel_id=1, source_target_pairs={{0,4},{2,6},{4,0},{6,2},{8,12},{10,14},{12,8},{14,10},{1,3},{3,1},... | collective-permute-start | bytes 294920 | tf_op jit(solution)/shard_map/ppermute | solution.py:178
  13.8 1.4 %collective-permute-start.5 = (bf16[16,6144]{1,0:T(8,128)(2,1)S(1)}, bf16[16,6144]{1,0:T(8,128)(2,1)S(1)}, u32[]{:S(2)}, u32[]{:S(2)}) collective-permute-start(bf16[16,6144]{1,0:T(8,128)(2,1)S(1)} %join.1.rest_2_), channel_id=1, source_target_pairs={{0,2},{2,0},{4,6},{6,4},{8,10},{10,8},{12,14},{14,12},{1,5},{3,7},... | collective-permute-start | bytes 589832 | tf_op jit(solution)/shard_map/ppermute | solution.py:180
  15.2 1.2 %early.1 = (f32[384,128]{1,0:T(8,128)S(1)}, f32[8,128]{1,0:T(8,128)S(1)}) custom-call(bf16[384,4096]{1,0:T(8,128)(2,1)S(1)} %copy-done, f32[384,1]{1,0:T(8,128)S(1)} %squares.1, bf16[8,6144]{1,0:T(8,128)(2,1)S(1)} %pack.1.rest_0_, bf16[8,6144]{1,0:T(8,128)(2,1)S(1)} %collective-permute-done.3.rest_1_, bf16[16,6144]{1,0:T(8,128)(2,1)S(1)} %join.1.rest_2_), custom_call_target="tpu_custom_call" | custom-call | flops 20000000000 | bytes 4194304 | tf_op jit(solution)/shard_map/early/pallas_call | solution.py:140
  16.4 0.2 collective-permute-done.rest_0_
  16.7 1.4 %collective-permute-done.4.rest_1_ = bf16[8,6144]{1,0:T(8,128)(2,1)S(1)} collective-permute-done((bf16[8,6144]{1,0:T(8,128)(2,1)S(1)}, bf16[8,6144]{1,0:T(8,128)(2,1)S(1)}, u32[]{:S(2)}, u32[]{:S(2)}) %collective-permute-start.4) | collective-permute-done | bytes 98336 | tf_op jit(solution)/shard_map/ppermute | solution.py:178
  18.1 1.4 %collective-permute-done.5.rest_2_ = bf16[16,6144]{1,0:T(8,128)(2,1)S(1)} collective-permute-done((bf16[16,6144]{1,0:T(8,128)(2,1)S(1)}, bf16[16,6144]{1,0:T(8,128)(2,1)S(1)}, u32[]{:S(2)}, u32[]{:S(2)}) %collective-permute-start.5) | collective-permute-done | bytes 196640 | tf_op jit(solution)/shard_map/ppermute | solution.py:180
  19.5 0.8 %late.3 = f32[200,128]{1,0:T(8,128)S(1)} custom-call(bf16[384,4096]{1,0:T(8,128)(2,1)S(1)} %copy-done, bf16[8,6144]{1,0:T(8,128)(2,1)S(1)} %collective-permute-done.rest_0_, bf16[8,6144]{1,0:T(8,128)(2,1)S(1)} %collective-permute-done.4.rest_1_, bf16[16,6144]{1,0:T(8,128)(2,1)S(1)} %collective-permute-done.5.rest_2_, ...), custom_call_target="tpu_custom_call" | custom-call | flops 1000000000 | bytes 4194304 | tf_op jit(solution)/shard_map/late/pallas_call | solution.py:140
  20.3 0.1 collective-permute-start.6
  20.4 0.8 %late.2.keep = f32[200,128]{1,0:T(8,128)S(1)} custom-call(bf16[384,4096]{1,0:T(8,128)(2,1)S(1)} %copy-done, bf16[8,6144]{1,0:T(8,128)(2,1)S(1)} %collective-permute-done.rest_0_, bf16[8,6144]{1,0:T(8,128)(2,1)S(1)} %collective-permute-done.4.rest_1_, bf16[16,6144]{1,0:T(8,128)(2,1)S(1)} %collective-permute-done.5.rest_2_, ...), custom_call_target="tpu_custom_call" | custom-call | flops 1000000000 | bytes 4194304 | tf_op jit(solution)/shard_map/late/pallas_call | solution.py:140
  21.2 0.5 %collective-permute-done.6.got = f32[200,128]{1,0:T(8,128)S(1)} collective-permute-done((f32[200,128]{1,0:T(8,128)S(1)}, f32[200,128]{1,0:T(8,128)S(1)}, u32[]{:S(2)}, u32[]{:S(2)}) %collective-permute-start.6) | collective-permute-done | bytes 102432 | tf_op jit(solution)/shard_map/ppermute | solution.py:208
  21.7 1.0 %finish.1 = f32[192,96]{1,0:T(8,128)} custom-call(f32[200,128]{1,0:T(8,128)S(1)} %late.2.keep, f32[200,128]{1,0:T(8,128)S(1)} %collective-permute-done.6.got), custom_call_target="tpu_custom_call" | custom-call | flops 1000000000 | bytes 4194304 | tf_op jit(solution)/shard_map/finish/pallas_call | solution.py:140
  (3 shorter events, 0.0 us)
Async XLA Ops:
  0.0 9.2 %copy-start = (bf16[384,4096]{1,0:T(8,128)(2,1)S(1)}, bf16[384,4096]{1,0:T(8,128)(2,1)}, u32[]{:S(2)}) copy-start(bf16[384,4096]{1,0:T(8,128)(2,1)} %documents.7) | copy-start | bytes 9437188
  0.0 1.1 %copy-start.1 = (bf16[12,4096]{1,0:T(8,128)(2,1)S(1)}, bf16[12,4096]{1,0:T(8,128)(2,1)}, u32[]{:S(2)}) copy-start(bf16[12,4096]{1,0:T(8,128)(2,1)} %queries_hbm.1) | copy-start | bytes 294916
  1.1 0.7 %copy-start.2 = (f32[4096]{0:T(1024)S(1)}, f32[4096]{0:T(1024)}, u32[]{:S(2)}) copy-start(f32[4096]{0:T(1024)} %param.5) | copy-start | bytes 49156
  2.0 9.2 %collective-permute-start.1 = (bf16[8,6144]{1,0:T(8,128)(2,1)S(1)}, bf16[8,6144]{1,0:T(8,128)(2,1)S(1)}, u32[]{:S(2)}, u32[]{:S(2)}) collective-permute-start(bf16[8,6144]{1,0:T(8,128)(2,1)S(1)} %pack.1.rest_0_), channel_id=1, source_target_pairs={{0,8},{2,10},{4,12},{6,14},{8,0},{10,2},{12,4},{14,6},{1,9},{3,11}... | collective-permute-start | bytes 294920 | tf_op jit(solution)/shard_map/ppermute | solution.py:172
  6.1 6.3 %collective-permute-start.2 = (bf16[8,6144]{1,0:T(8,128)(2,1)S(1)}, bf16[8,6144]{1,0:T(8,128)(2,1)S(1)}, u32[]{:S(2)}, u32[]{:S(2)}) collective-permute-start(bf16[8,6144]{1,0:T(8,128)(2,1)S(1)} %pack.1.rest_0_), channel_id=1, source_target_pairs={{0,4},{2,6},{4,0},{6,2},{8,12},{10,14},{12,8},{14,10},{1,3},{3,1},... | collective-permute-start | bytes 294920 | tf_op jit(solution)/shard_map/ppermute | solution.py:173
  7.7 4.8 %collective-permute-start.3 = (bf16[8,6144]{1,0:T(8,128)(2,1)S(1)}, bf16[8,6144]{1,0:T(8,128)(2,1)S(1)}, u32[]{:S(2)}, u32[]{:S(2)}) collective-permute-start(bf16[8,6144]{1,0:T(8,128)(2,1)S(1)} %pack.1.rest_0_), channel_id=1, source_target_pairs={{0,2},{2,0},{4,6},{6,4},{8,10},{10,8},{12,14},{14,12},{1,5},{3,7},... | collective-permute-start | bytes 294920 | tf_op jit(solution)/shard_map/ppermute | solution.py:174
  9.2 7.5 %collective-permute-start = (bf16[8,6144]{1,0:T(8,128)(2,1)S(1)}, bf16[8,6144]{1,0:T(8,128)(2,1)S(1)}, u32[]{:S(2)}, u32[]{:S(2)}) collective-permute-start(bf16[8,6144]{1,0:T(8,128)(2,1)S(1)} %pack.1.rest_0_), channel_id=1, source_target_pairs={{0,14},{2,12},{4,10},{6,8},{8,6},{10,4},{12,2},{14,0},{1,15},{3,13... | collective-permute-start | bytes 294920 | tf_op jit(solution)/shard_map/ppermute | solution.py:175
  12.4 5.7 %collective-permute-start.4 = (bf16[8,6144]{1,0:T(8,128)(2,1)S(1)}, bf16[8,6144]{1,0:T(8,128)(2,1)S(1)}, u32[]{:S(2)}, u32[]{:S(2)}) collective-permute-start(bf16[8,6144]{1,0:T(8,128)(2,1)S(1)} %collective-permute-done.1.second), channel_id=1, source_target_pairs={{0,4},{2,6},{4,0},{6,2},{8,12},{10,14},{12,8},{14,10},{1,3},{3,1},... | collective-permute-start | bytes 294920 | tf_op jit(solution)/shard_map/ppermute | solution.py:178
  13.8 5.7 %collective-permute-start.5 = (bf16[16,6144]{1,0:T(8,128)(2,1)S(1)}, bf16[16,6144]{1,0:T(8,128)(2,1)S(1)}, u32[]{:S(2)}, u32[]{:S(2)}) collective-permute-start(bf16[16,6144]{1,0:T(8,128)(2,1)S(1)} %join.1.rest_2_), channel_id=1, source_target_pairs={{0,2},{2,0},{4,6},{6,4},{8,10},{10,8},{12,14},{14,12},{1,5},{3,7},... | collective-permute-start | bytes 589832 | tf_op jit(solution)/shard_map/ppermute | solution.py:180
  20.3 1.4 %collective-permute-start.6 = (f32[200,128]{1,0:T(8,128)S(1)}, f32[200,128]{1,0:T(8,128)S(1)}, u32[]{:S(2)}, u32[]{:S(2)}) collective-permute-start(f32[200,128]{1,0:T(8,128)S(1)} %late.3), channel_id=1, source_target_pairs={{0,1},{1,0},{2,3},{3,2},{4,5},{5,4},{6,7},{7,6},{8,9},{9,8},{10,11... | collective-permute-start | bytes 307208 | tf_op jit(solution)/shard_map/ppermute | solution.py:208

commit v3 on v2

--- a/solution.py
+++ b/solution.py
@@ -162,7 +162,7 @@
         queries,
         preconditioner.reshape(1, width),
         hbm=True,
-        limit=24,
+        limit=56,
         scratch=[
             pltpu.VMEM(queries.shape, queries.dtype),
             pltpu.VMEM((1, width), jnp.float32),
@@ -174,7 +174,7 @@
     n2 = lax.ppermute(packed, BOTH, second)
     corner = lax.ppermute(packed, "blk", farthest)
     squares = call(squares_kernel, "squares", pltpu.VMEM((docs, 1), jnp.float32), documents)
-    across, n1, n2, squares = lax.optimization_barrier((across, n1, n2, squares))
+    across, squares = lax.optimization_barrier((across, squares))
     a1 = lax.ppermute(across, BOTH, first)
     two = call(join_kernel, "join", pltpu.VMEM((16, 3 * width // 2), jnp.bfloat16), n1, across)
     pair = lax.ppermute(two, BOTH, second)

time: 22.9 us -> 21.1 us (0.921)
  local copies, waits for them, and re-layouts: 1.77 us -> 0.01 us
  Pallas kernels: 4.65 us -> 5.48 us
  starting transfers between devices: 10 us -> 9.24 us
    unnamed x6 -> x2, local copies, waits for them, and re-layouts: 1.77 us -> 0.01 us
    ppermute x1, waiting for transfers between devices: 0.23 us -> 1.72 us  [by_squares(): corner = lax.ppermute(packed, 'blk', farthest)]
    pallas_call x7, Pallas kernels: 4.65 us -> 5.48 us  [call(): pl.pallas_call(kernel, out_shape=out, in_specs=[anywhere() if hbm else vm...]
    ppermute x1, starting transfers between devices: 1.37 us -> 0.64 us  [by_squares(): a1 = lax.ppermute(across, BOTH, first)]
    ppermute x1, waiting for transfers between devices: 1.21 us -> 0.57 us  [by_squares(): n1 = lax.ppermute(packed, BOTH, first)]
    ppermute x1, waiting for transfers between devices: 1.45 us -> 0.99 us  [by_squares(): pair = lax.ppermute(two, BOTH, second)]
    ppermute x1, waiting for transfers between devices: 1.43 us -> 1.05 us  [by_squares(): a1 = lax.ppermute(across, BOTH, first)]
  transfers between devices with their start and end apart: 7 -> 7, of which waited for: 6 -> 6; matrix products, arithmetic and copies ran while one was open for 0% -> 0% of each run, Pallas kernels for 12% -> 13%
where the time goes in v3:
time: 21.1 us; the launch traced here: 21 us
  starting transfers between devices  9.24 us (44%)
  waiting for transfers between devices  6.2 us (29%)
  Pallas kernels  5.48 us (26%)
    pallas_call x7, Pallas kernels, call(): pl.pallas_call(kernel, out_shape=out, in_specs=[anywhere() if hbm else vm...  5.48 us
    ppermute x1, starting transfers between devices, by_squares(): across = lax.ppermute(packed, 'blk', far)  4.1 us
    ppermute x1, waiting for transfers between devices, by_squares(): corner = lax.ppermute(packed, 'blk', farthest)  1.72 us
    ppermute x1, starting transfers between devices, by_squares(): n1 = lax.ppermute(packed, BOTH, first)  1.58 us
    ppermute x1, starting transfers between devices, by_squares(): n2 = lax.ppermute(packed, BOTH, second)  1.49 us
    ppermute x1, starting transfers between devices, by_squares(): pair = lax.ppermute(two, BOTH, second)  1.35 us
    ppermute x1, waiting for transfers between devices, by_squares(): across = lax.ppermute(packed, 'blk', far)  1.35 us
    ppermute x1, waiting for transfers between devices, by_squares(): a1 = lax.ppermute(across, BOTH, first)  1.05 us
  transfers between devices with their start and end apart: 7, of which 6 were waited for; matrix products, arithmetic and copies ran while one was open for 0% of the time, Pallas kernels for 13%

profile of v3, /device:TPU:0, one launch (start us, length us, event | category | flops | bytes accessed | tf_op | source)
XLA Modules:
  0.0 21.0 jit_solution(13439430413508214393)
XLA Ops:
  0.0 0.0 copy-start
  0.0 1.1 %pack.1.rest_0_ = bf16[8,6144]{1,0:T(8,128)(2,1)S(1)} custom-call(bf16[12,4096]{1,0:T(8,128)(2,1)} %queries_hbm.1, f32[1,4096]{1,0:T(1,128)} %bitcast.1), custom_call_target="tpu_custom_call" | custom-call | flops 1000000000 | bytes 4194304 | tf_op jit(solution)/shard_map/pack/pallas_call | solution.py:140
  1.1 4.1 %collective-permute-start.1 = (bf16[8,6144]{1,0:T(8,128)(2,1)S(1)}, bf16[8,6144]{1,0:T(8,128)(2,1)S(1)}, u32[]{:S(2)}, u32[]{:S(2)}) collective-permute-start(bf16[8,6144]{1,0:T(8,128)(2,1)S(1)} %pack.1.rest_0_), channel_id=1, source_target_pairs={{0,8},{2,10},{4,12},{6,14},{8,0},{10,2},{12,4},{14,6},{1,9},{3,11}... | collective-permute-start | bytes 294920 | tf_op jit(solution)/shard_map/ppermute | solution.py:172
  5.2 1.6 %collective-permute-start.3 = (bf16[8,6144]{1,0:T(8,128)(2,1)S(1)}, bf16[8,6144]{1,0:T(8,128)(2,1)S(1)}, u32[]{:S(2)}, u32[]{:S(2)}) collective-permute-start(bf16[8,6144]{1,0:T(8,128)(2,1)S(1)} %pack.1.rest_0_), channel_id=1, source_target_pairs={{0,4},{2,6},{4,0},{6,2},{8,12},{10,14},{12,8},{14,10},{1,3},{3,1},... | collective-permute-start | bytes 294920 | tf_op jit(solution)/shard_map/ppermute | solution.py:173
  6.8 1.5 %collective-permute-start.5 = (bf16[8,6144]{1,0:T(8,128)(2,1)S(1)}, bf16[8,6144]{1,0:T(8,128)(2,1)S(1)}, u32[]{:S(2)}, u32[]{:S(2)}) collective-permute-start(bf16[8,6144]{1,0:T(8,128)(2,1)S(1)} %pack.1.rest_0_), channel_id=1, source_target_pairs={{0,2},{2,0},{4,6},{6,4},{8,10},{10,8},{12,14},{14,12},{1,5},{3,7},... | collective-permute-start | bytes 294920 | tf_op jit(solution)/shard_map/ppermute | solution.py:174
  8.3 0.0 collective-permute-start
  8.3 0.0 copy-done
  8.3 0.7 %squares.1 = f32[384,1]{1,0:T(8,128)S(1)} custom-call(bf16[384,4096]{1,0:T(8,128)(2,1)S(1)} %copy-done), custom_call_target="tpu_custom_call" | custom-call | flops 20000000000 | bytes 4194304 | tf_op jit(solution)/shard_map/squares/pallas_call | solution.py:140
  9.0 1.3 %collective-permute-done.1.second = bf16[8,6144]{1,0:T(8,128)(2,1)S(1)} collective-permute-done((bf16[8,6144]{1,0:T(8,128)(2,1)S(1)}, bf16[8,6144]{1,0:T(8,128)(2,1)S(1)}, u32[]{:S(2)}, u32[]{:S(2)}) %collective-permute-start.1) | collective-permute-done | bytes 98336 | tf_op jit(solution)/shard_map/ppermute | solution.py:172
  10.3 0.6 %collective-permute-start.2 = (bf16[8,6144]{1,0:T(8,128)(2,1)S(1)}, bf16[8,6144]{1,0:T(8,128)(2,1)S(1)}, u32[]{:S(2)}, u32[]{:S(2)}) collective-permute-start(bf16[8,6144]{1,0:T(8,128)(2,1)S(1)} %collective-permute-done.1.second), channel_id=1, source_target_pairs={{0,4},{2,6},{4,0},{6,2},{8,12},{10,14},{12,8},{14,10},{1,3},{3,1},... | collective-permute-start | bytes 294920 | tf_op jit(solution)/shard_map/ppermute | solution.py:178
  11.0 0.6 %collective-permute-done.3.first = bf16[8,6144]{1,0:T(8,128)(2,1)S(1)} collective-permute-done((bf16[8,6144]{1,0:T(8,128)(2,1)S(1)}, bf16[8,6144]{1,0:T(8,128)(2,1)S(1)}, u32[]{:S(2)}, u32[]{:S(2)}) %collective-permute-start.3) | collective-permute-done | bytes 98336 | tf_op jit(solution)/shard_map/ppermute | solution.py:173
  11.6 1.3 %collective-permute-start.4 = (bf16[16,6144]{1,0:T(8,128)(2,1)S(1)}, bf16[16,6144]{1,0:T(8,128)(2,1)S(1)}, u32[]{:S(2)}, u32[]{:S(2)}) collective-permute-start(bf16[16,6144]{1,0:T(8,128)(2,1)S(1)} %join.1.rest_2_), channel_id=1, source_target_pairs={{0,2},{2,0},{4,6},{6,4},{8,10},{10,8},{12,14},{14,12},{1,5},{3,7},... | collective-permute-start | bytes 589832 | tf_op jit(solution)/shard_map/ppermute | solution.py:180
  12.9 0.0 collective-permute-done.5.rest_1_
  12.9 1.2 %early.1 = (f32[384,128]{1,0:T(8,128)S(1)}, f32[8,128]{1,0:T(8,128)S(1)}) custom-call(bf16[384,4096]{1,0:T(8,128)(2,1)S(1)} %copy-done, f32[384,1]{1,0:T(8,128)S(1)} %squares.1, bf16[8,6144]{1,0:T(8,128)(2,1)S(1)} %pack.1.rest_0_, bf16[8,6144]{1,0:T(8,128)(2,1)S(1)} %collective-permute-done.5.rest_1_, bf16[16,6144]{1,0:T(8,128)(2,1)S(1)} %join.1.rest_2_), custom_call_target="tpu_custom_call" | custom-call | flops 20000000000 | bytes 4194304 | tf_op jit(solution)/shard_map/early/pallas_call | solution.py:140
  14.1 1.7 %collective-permute-done.rest_0_ = bf16[8,6144]{1,0:T(8,128)(2,1)S(1)} collective-permute-done((bf16[8,6144]{1,0:T(8,128)(2,1)S(1)}, bf16[8,6144]{1,0:T(8,128)(2,1)S(1)}, u32[]{:S(2)}, u32[]{:S(2)}) %collective-permute-start) | collective-permute-done | bytes 98336 | tf_op jit(solution)/shard_map/ppermute | solution.py:175
  15.8 1.1 %collective-permute-done.2.rest_1_ = bf16[8,6144]{1,0:T(8,128)(2,1)S(1)} collective-permute-done((bf16[8,6144]{1,0:T(8,128)(2,1)S(1)}, bf16[8,6144]{1,0:T(8,128)(2,1)S(1)}, u32[]{:S(2)}, u32[]{:S(2)}) %collective-permute-start.2) | collective-permute-done | bytes 98336 | tf_op jit(solution)/shard_map/ppermute | solution.py:178
  16.9 1.0 %collective-permute-done.4.rest_2_ = bf16[16,6144]{1,0:T(8,128)(2,1)S(1)} collective-permute-done((bf16[16,6144]{1,0:T(8,128)(2,1)S(1)}, bf16[16,6144]{1,0:T(8,128)(2,1)S(1)}, u32[]{:S(2)}, u32[]{:S(2)}) %collective-permute-start.4) | collective-permute-done | bytes 196640 | tf_op jit(solution)/shard_map/ppermute | solution.py:180
  17.9 0.8 %late.3 = f32[200,128]{1,0:T(8,128)S(1)} custom-call(bf16[384,4096]{1,0:T(8,128)(2,1)S(1)} %copy-done, bf16[8,6144]{1,0:T(8,128)(2,1)S(1)} %collective-permute-done.rest_0_, bf16[8,6144]{1,0:T(8,128)(2,1)S(1)} %collective-permute-done.2.rest_1_, bf16[16,6144]{1,0:T(8,128)(2,1)S(1)} %collective-permute-done.4.rest_2_, ...), custom_call_target="tpu_custom_call" | custom-call | flops 1000000000 | bytes 4194304 | tf_op jit(solution)/shard_map/late/pallas_call | solution.py:140
  18.6 0.1 collective-permute-start.6
  18.7 0.8 %late.2.keep = f32[200,128]{1,0:T(8,128)S(1)} custom-call(bf16[384,4096]{1,0:T(8,128)(2,1)S(1)} %copy-done, bf16[8,6144]{1,0:T(8,128)(2,1)S(1)} %collective-permute-done.rest_0_, bf16[8,6144]{1,0:T(8,128)(2,1)S(1)} %collective-permute-done.2.rest_1_, bf16[16,6144]{1,0:T(8,128)(2,1)S(1)} %collective-permute-done.4.rest_2_, ...), custom_call_target="tpu_custom_call" | custom-call | flops 1000000000 | bytes 4194304 | tf_op jit(solution)/shard_map/late/pallas_call | solution.py:140
  19.5 0.5 %collective-permute-done.6.got = f32[200,128]{1,0:T(8,128)S(1)} collective-permute-done((f32[200,128]{1,0:T(8,128)S(1)}, f32[200,128]{1,0:T(8,128)S(1)}, u32[]{:S(2)}, u32[]{:S(2)}) %collective-permute-start.6) | collective-permute-done | bytes 102432 | tf_op jit(solution)/shard_map/ppermute | solution.py:208
  20.0 1.0 %finish.1 = f32[192,96]{1,0:T(8,128)} custom-call(f32[200,128]{1,0:T(8,128)S(1)} %late.2.keep, f32[200,128]{1,0:T(8,128)S(1)} %collective-permute-done.6.got), custom_call_target="tpu_custom_call" | custom-call | flops 1000000000 | bytes 4194304 | tf_op jit(solution)/shard_map/finish/pallas_call | solution.py:140
  (1 shorter events, 0.0 us)
Async XLA Ops:
  0.0 8.3 %copy-start = (bf16[384,4096]{1,0:T(8,128)(2,1)S(1)}, bf16[384,4096]{1,0:T(8,128)(2,1)}, u32[]{:S(2)}) copy-start(bf16[384,4096]{1,0:T(8,128)(2,1)} %documents.7) | copy-start | bytes 9437188
  1.1 9.2 %collective-permute-start.1 = (bf16[8,6144]{1,0:T(8,128)(2,1)S(1)}, bf16[8,6144]{1,0:T(8,128)(2,1)S(1)}, u32[]{:S(2)}, u32[]{:S(2)}) collective-permute-start(bf16[8,6144]{1,0:T(8,128)(2,1)S(1)} %pack.1.rest_0_), channel_id=1, source_target_pairs={{0,8},{2,10},{4,12},{6,14},{8,0},{10,2},{12,4},{14,6},{1,9},{3,11}... | collective-permute-start | bytes 294920 | tf_op jit(solution)/shard_map/ppermute | solution.py:172
  5.2 6.3 %collective-permute-start.3 = (bf16[8,6144]{1,0:T(8,128)(2,1)S(1)}, bf16[8,6144]{1,0:T(8,128)(2,1)S(1)}, u32[]{:S(2)}, u32[]{:S(2)}) collective-permute-start(bf16[8,6144]{1,0:T(8,128)(2,1)S(1)} %pack.1.rest_0_), channel_id=1, source_target_pairs={{0,4},{2,6},{4,0},{6,2},{8,12},{10,14},{12,8},{14,10},{1,3},{3,1},... | collective-permute-start | bytes 294920 | tf_op jit(solution)/shard_map/ppermute | solution.py:173
  6.8 6.1 %collective-permute-start.5 = (bf16[8,6144]{1,0:T(8,128)(2,1)S(1)}, bf16[8,6144]{1,0:T(8,128)(2,1)S(1)}, u32[]{:S(2)}, u32[]{:S(2)}) collective-permute-start(bf16[8,6144]{1,0:T(8,128)(2,1)S(1)} %pack.1.rest_0_), channel_id=1, source_target_pairs={{0,2},{2,0},{4,6},{6,4},{8,10},{10,8},{12,14},{14,12},{1,5},{3,7},... | collective-permute-start | bytes 294920 | tf_op jit(solution)/shard_map/ppermute | solution.py:174
  8.3 7.5 %collective-permute-start = (bf16[8,6144]{1,0:T(8,128)(2,1)S(1)}, bf16[8,6144]{1,0:T(8,128)(2,1)S(1)}, u32[]{:S(2)}, u32[]{:S(2)}) collective-permute-start(bf16[8,6144]{1,0:T(8,128)(2,1)S(1)} %pack.1.rest_0_), channel_id=1, source_target_pairs={{0,14},{2,12},{4,10},{6,8},{8,6},{10,4},{12,2},{14,0},{1,15},{3,13... | collective-permute-start | bytes 294920 | tf_op jit(solution)/shard_map/ppermute | solution.py:175
  10.3 6.5 %collective-permute-start.2 = (bf16[8,6144]{1,0:T(8,128)(2,1)S(1)}, bf16[8,6144]{1,0:T(8,128)(2,1)S(1)}, u32[]{:S(2)}, u32[]{:S(2)}) collective-permute-start(bf16[8,6144]{1,0:T(8,128)(2,1)S(1)} %collective-permute-done.1.second), channel_id=1, source_target_pairs={{0,4},{2,6},{4,0},{6,2},{8,12},{10,14},{12,8},{14,10},{1,3},{3,1},... | collective-permute-start | bytes 294920 | tf_op jit(solution)/shard_map/ppermute | solution.py:178
  11.6 6.3 %collective-permute-start.4 = (bf16[16,6144]{1,0:T(8,128)(2,1)S(1)}, bf16[16,6144]{1,0:T(8,128)(2,1)S(1)}, u32[]{:S(2)}, u32[]{:S(2)}) collective-permute-start(bf16[16,6144]{1,0:T(8,128)(2,1)S(1)} %join.1.rest_2_), channel_id=1, source_target_pairs={{0,2},{2,0},{4,6},{6,4},{8,10},{10,8},{12,14},{14,12},{1,5},{3,7},... | collective-permute-start | bytes 589832 | tf_op jit(solution)/shard_map/ppermute | solution.py:180
  18.6 1.4 %collective-permute-start.6 = (f32[200,128]{1,0:T(8,128)S(1)}, f32[200,128]{1,0:T(8,128)S(1)}, u32[]{:S(2)}, u32[]{:S(2)}) collective-permute-start(f32[200,128]{1,0:T(8,128)S(1)} %late.3), channel_id=1, source_target_pairs={{0,1},{1,0},{2,3},{3,2},{4,5},{5,4},{6,7},{7,6},{8,9},{9,8},{10,11... | collective-permute-start | bytes 307208 | tf_op jit(solution)/shard_map/ppermute | solution.py:208

commit v4 on v3

--- a/solution.py
+++ b/solution.py
@@ -12,6 +12,7 @@
 MIB = 1024 * 1024
 BOTH = ("blk", "proj")
 NT = (((1,), (1,)), ((), ()))
+SQUARES_LANE = 96
 
 
 def vmem():
@@ -64,19 +65,21 @@
     return jnp.concatenate([packed[:, :width], jnp.concatenate([tail, tail], axis=1)], axis=0)
 
 
-def scatter(places, pieces, whole):
-    whole[...] = jnp.zeros_like(whole)
-    for place, piece in zip(places, pieces):
-        whole[pl.ds(pl.multiple_of(place * 16, 16), 16), :] = unpack(piece)
-
-
-def products(left, whole):
+def products(left, pieces, places, whole):
+    for slot, piece in enumerate(pieces):
+        whole[16 * slot : 16 * slot + 16, :] = unpack(piece)
     middle = whole.shape[1] // 2
     low = lax.dot_general(left[:, :middle], whole[:, :middle], NT, preferred_element_type=jnp.float32)
     high = lax.dot_general(left[:, middle:], whole[:, middle:], NT, preferred_element_type=jnp.float32)
-    lane = lax.broadcasted_iota(jnp.int32, low.shape, 1) & 15
-    moved = pltpu.roll(high, low.shape[1] - 4, 1)
-    return jnp.where(lane < 8, low + high, jnp.where(lane < 12, low + moved, 0.0))
+    lanes = low.shape[1]
+    lane = lax.broadcasted_iota(jnp.int32, low.shape, 1)
+    moved = pltpu.roll(high, lanes - 4, 1)
+    both = jnp.where(lane & 15 < 8, low + high, low + moved)
+    total = jnp.zeros(low.shape, jnp.float32)
+    for slot, place in enumerate(places):
+        placed = pltpu.roll(both, (12 * place - 16 * slot + lanes) % lanes, 1)
+        total = jnp.where((lane >= 12 * place) & (lane < 12 * place + 12), placed, total)
+    return total
 
 
 def own_squares(places, pieces, lanes):
@@ -89,41 +92,41 @@
         wide = wide * wide
         head = jnp.sum(wide[:, :width], axis=1, keepdims=True)
         tail = jnp.sum(wide[:, width:], axis=1, keepdims=True)
-        total += jnp.where(lane == place * 16 + row, head, 0.0)
-        total += jnp.where(lane == place * 16 + 8 + (row & 3), tail, 0.0)
+        total += jnp.where(lane == place * 12 + row, head, 0.0)
+        total += jnp.where(lane == place * 12 + 8 + (row & 3), tail, 0.0)
     return jnp.broadcast_to(jnp.sum(total, axis=0, keepdims=True), (8, lanes))
+
+
+def parts(refs):
+    return [ref[r : r + 8] for ref in refs for r in range(0, ref.shape[0], 8)]
 
 
 def early_kernel(steps, documents, squares, *rest):
     refs, (scores, query_squares, whole) = rest[:-3], rest[-3:]
-    places, pieces = blocks_from(steps), [ref[r : r + 8] for ref in refs for r in range(0, ref.shape[0], 8)]
-    scatter(places, pieces, whole)
+    places, pieces = blocks_from(steps), parts(refs)
     lane = lax.broadcasted_iota(jnp.int32, scores.shape, 1)
-    scores[...] = jnp.where(lane == 12, squares[...], products(documents, whole))
+    raw = products(documents, pieces, places, whole)
+    scores[...] = jnp.where(lane == SQUARES_LANE, squares[...], raw)
     query_squares[...] = own_squares(places, pieces, scores.shape[1])
 
 
 def late_kernel(steps, other, documents, *rest):
     refs, (scores, query_squares, out, whole) = rest[:-4], rest[-4:]
     half = out.shape[0] - 8
-    places, pieces = blocks_from(steps), [ref[r : r + 8] for ref in refs for r in range(0, ref.shape[0], 8)]
-    scatter(places, pieces, whole)
+    places, pieces = blocks_from(steps), parts(refs)
     core = lax.axis_index("proj")
     side = 1 - core if other else core
     rows = pl.ds(pl.multiple_of(side * half, 16), half)
-    out[:half, :] = scores[rows, :] + products(documents.at[rows], whole)
+    out[:half, :] = scores[rows, :] + products(documents.at[rows], pieces, places, whole)
     out[half:, :] = query_squares[...] + own_squares(places, pieces, out.shape[1])
 
 
 def finish_kernel(coordinates, keep, got, scores):
-    half = scores.shape[0]
+    half, width = scores.shape
     total = keep[...] + got[...]
-    doc_scale = lax.rsqrt(total[:half, 12:13] / coordinates + EPS)
+    doc_scale = lax.rsqrt(total[:half, SQUARES_LANE : SQUARES_LANE + 1] / coordinates + EPS)
     query_scale = lax.rsqrt(total[half : half + 1, :] / coordinates + EPS) / math.sqrt(coordinates)
-    scaled = total[:half] * doc_scale * query_scale
-    scores[...] = jnp.concatenate(
-        [scaled[:, 16 * j : 16 * j + 12] for j in range(scores.shape[1] // 12)], axis=1
-    )
+    scores[...] = (total[:half] * doc_scale * query_scale)[:, :width]
 
 
 def squared_paths(blocks):

time: 21.1 us -> 20.9 us (level)
  no operation moved by 1% of the time
where the time goes in v4:
time: 20.9 us; the launch traced here: 20.8 us
  starting transfers between devices  9.24 us (44%)
  waiting for transfers between devices  6.16 us (29%)
  Pallas kernels  5.31 us (25%)
    pallas_call x7, Pallas kernels, call(): pl.pallas_call(kernel, out_shape=out, in_specs=[anywhere() if hbm else vm...  5.31 us
    ppermute x1, starting transfers between devices, by_squares(): across = lax.ppermute(packed, 'blk', far)  4.1 us
    ppermute x1, waiting for transfers between devices, by_squares(): corner = lax.ppermute(packed, 'blk', farthest)  1.66 us
    ppermute x1, starting transfers between devices, by_squares(): n1 = lax.ppermute(packed, BOTH, first)  1.58 us
    ppermute x1, starting transfers between devices, by_squares(): n2 = lax.ppermute(packed, BOTH, second)  1.49 us
    ppermute x1, starting transfers between devices, by_squares(): pair = lax.ppermute(two, BOTH, second)  1.35 us
    ppermute x1, waiting for transfers between devices, by_squares(): across = lax.ppermute(packed, 'blk', far)  1.35 us
    ppermute x1, waiting for transfers between devices, by_squares(): a1 = lax.ppermute(across, BOTH, first)  1.05 us
  transfers between devices with their start and end apart: 7, of which 6 were waited for; matrix products, arithmetic and copies ran while one was open for 0% of the time, Pallas kernels for 13%

profile of v4, /device:TPU:0, one launch (start us, length us, event | category | flops | bytes accessed | tf_op | source)
XLA Modules:
  0.0 20.8 jit_solution(302659862115839534)
XLA Ops:
  0.0 0.0 copy-start
  0.0 1.1 %pack.1.rest_0_ = bf16[8,6144]{1,0:T(8,128)(2,1)S(1)} custom-call(bf16[12,4096]{1,0:T(8,128)(2,1)} %queries_hbm.1, f32[1,4096]{1,0:T(1,128)} %bitcast.1), custom_call_target="tpu_custom_call" | custom-call | flops 1000000000 | bytes 4194304 | tf_op jit(solution)/shard_map/pack/pallas_call | solution.py:143
  1.1 4.1 %collective-permute-start.1 = (bf16[8,6144]{1,0:T(8,128)(2,1)S(1)}, bf16[8,6144]{1,0:T(8,128)(2,1)S(1)}, u32[]{:S(2)}, u32[]{:S(2)}) collective-permute-start(bf16[8,6144]{1,0:T(8,128)(2,1)S(1)} %pack.1.rest_0_), channel_id=1, source_target_pairs={{0,8},{2,10},{4,12},{6,14},{8,0},{10,2},{12,4},{14,6},{1,9},{3,11}... | collective-permute-start | bytes 294920 | tf_op jit(solution)/shard_map/ppermute | solution.py:175
  5.2 1.6 %collective-permute-start.3 = (bf16[8,6144]{1,0:T(8,128)(2,1)S(1)}, bf16[8,6144]{1,0:T(8,128)(2,1)S(1)}, u32[]{:S(2)}, u32[]{:S(2)}) collective-permute-start(bf16[8,6144]{1,0:T(8,128)(2,1)S(1)} %pack.1.rest_0_), channel_id=1, source_target_pairs={{0,4},{2,6},{4,0},{6,2},{8,12},{10,14},{12,8},{14,10},{1,3},{3,1},... | collective-permute-start | bytes 294920 | tf_op jit(solution)/shard_map/ppermute | solution.py:176
  6.8 1.5 %collective-permute-start.5 = (bf16[8,6144]{1,0:T(8,128)(2,1)S(1)}, bf16[8,6144]{1,0:T(8,128)(2,1)S(1)}, u32[]{:S(2)}, u32[]{:S(2)}) collective-permute-start(bf16[8,6144]{1,0:T(8,128)(2,1)S(1)} %pack.1.rest_0_), channel_id=1, source_target_pairs={{0,2},{2,0},{4,6},{6,4},{8,10},{10,8},{12,14},{14,12},{1,5},{3,7},... | collective-permute-start | bytes 294920 | tf_op jit(solution)/shard_map/ppermute | solution.py:177
  8.3 0.0 collective-permute-start
  8.3 0.0 copy-done
  8.3 0.7 %squares.1 = f32[384,1]{1,0:T(8,128)S(1)} custom-call(bf16[384,4096]{1,0:T(8,128)(2,1)S(1)} %copy-done), custom_call_target="tpu_custom_call" | custom-call | flops 20000000000 | bytes 4194304 | tf_op jit(solution)/shard_map/squares/pallas_call | solution.py:143
  9.0 1.3 %collective-permute-done.1.second = bf16[8,6144]{1,0:T(8,128)(2,1)S(1)} collective-permute-done((bf16[8,6144]{1,0:T(8,128)(2,1)S(1)}, bf16[8,6144]{1,0:T(8,128)(2,1)S(1)}, u32[]{:S(2)}, u32[]{:S(2)}) %collective-permute-start.1) | collective-permute-done | bytes 98336 | tf_op jit(solution)/shard_map/ppermute | solution.py:175
  10.3 0.6 %collective-permute-start.2 = (bf16[8,6144]{1,0:T(8,128)(2,1)S(1)}, bf16[8,6144]{1,0:T(8,128)(2,1)S(1)}, u32[]{:S(2)}, u32[]{:S(2)}) collective-permute-start(bf16[8,6144]{1,0:T(8,128)(2,1)S(1)} %collective-permute-done.1.second), channel_id=1, source_target_pairs={{0,4},{2,6},{4,0},{6,2},{8,12},{10,14},{12,8},{14,10},{1,3},{3,1},... | collective-permute-start | bytes 294920 | tf_op jit(solution)/shard_map/ppermute | solution.py:181
  11.0 0.6 %collective-permute-done.3.first = bf16[8,6144]{1,0:T(8,128)(2,1)S(1)} collective-permute-done((bf16[8,6144]{1,0:T(8,128)(2,1)S(1)}, bf16[8,6144]{1,0:T(8,128)(2,1)S(1)}, u32[]{:S(2)}, u32[]{:S(2)}) %collective-permute-start.3) | collective-permute-done | bytes 98336 | tf_op jit(solution)/shard_map/ppermute | solution.py:176
  11.6 1.3 %collective-permute-start.4 = (bf16[16,6144]{1,0:T(8,128)(2,1)S(1)}, bf16[16,6144]{1,0:T(8,128)(2,1)S(1)}, u32[]{:S(2)}, u32[]{:S(2)}) collective-permute-start(bf16[16,6144]{1,0:T(8,128)(2,1)S(1)} %join.1.rest_2_), channel_id=1, source_target_pairs={{0,2},{2,0},{4,6},{6,4},{8,10},{10,8},{12,14},{14,12},{1,5},{3,7},... | collective-permute-start | bytes 589832 | tf_op jit(solution)/shard_map/ppermute | solution.py:183
  12.9 0.0 collective-permute-done.5.rest_1_
  12.9 1.2 %early.1 = (f32[384,128]{1,0:T(8,128)S(1)}, f32[8,128]{1,0:T(8,128)S(1)}) custom-call(bf16[384,4096]{1,0:T(8,128)(2,1)S(1)} %copy-done, f32[384,1]{1,0:T(8,128)S(1)} %squares.1, bf16[8,6144]{1,0:T(8,128)(2,1)S(1)} %pack.1.rest_0_, bf16[8,6144]{1,0:T(8,128)(2,1)S(1)} %collective-permute-done.5.rest_1_, bf16[16,6144]{1,0:T(8,128)(2,1)S(1)} %join.1.rest_2_), custom_call_target="tpu_custom_call" | custom-call | flops 20000000000 | bytes 4194304 | tf_op jit(solution)/shard_map/early/pallas_call | solution.py:143
  14.1 1.7 %collective-permute-done.rest_0_ = bf16[8,6144]{1,0:T(8,128)(2,1)S(1)} collective-permute-done((bf16[8,6144]{1,0:T(8,128)(2,1)S(1)}, bf16[8,6144]{1,0:T(8,128)(2,1)S(1)}, u32[]{:S(2)}, u32[]{:S(2)}) %collective-permute-start) | collective-permute-done | bytes 98336 | tf_op jit(solution)/shard_map/ppermute | solution.py:178
  15.8 1.1 %collective-permute-done.2.rest_1_ = bf16[8,6144]{1,0:T(8,128)(2,1)S(1)} collective-permute-done((bf16[8,6144]{1,0:T(8,128)(2,1)S(1)}, bf16[8,6144]{1,0:T(8,128)(2,1)S(1)}, u32[]{:S(2)}, u32[]{:S(2)}) %collective-permute-start.2) | collective-permute-done | bytes 98336 | tf_op jit(solution)/shard_map/ppermute | solution.py:181
  16.9 1.0 %collective-permute-done.4.rest_2_ = bf16[16,6144]{1,0:T(8,128)(2,1)S(1)} collective-permute-done((bf16[16,6144]{1,0:T(8,128)(2,1)S(1)}, bf16[16,6144]{1,0:T(8,128)(2,1)S(1)}, u32[]{:S(2)}, u32[]{:S(2)}) %collective-permute-start.4) | collective-permute-done | bytes 196640 | tf_op jit(solution)/shard_map/ppermute | solution.py:183
  17.9 0.8 %late.3 = f32[200,128]{1,0:T(8,128)S(1)} custom-call(bf16[384,4096]{1,0:T(8,128)(2,1)S(1)} %copy-done, bf16[8,6144]{1,0:T(8,128)(2,1)S(1)} %collective-permute-done.rest_0_, bf16[8,6144]{1,0:T(8,128)(2,1)S(1)} %collective-permute-done.2.rest_1_, bf16[16,6144]{1,0:T(8,128)(2,1)S(1)} %collective-permute-done.4.rest_2_, ...), custom_call_target="tpu_custom_call" | custom-call | flops 1000000000 | bytes 4194304 | tf_op jit(solution)/shard_map/late/pallas_call | solution.py:143
  18.6 0.1 collective-permute-start.6
  18.7 0.8 %late.2.keep = f32[200,128]{1,0:T(8,128)S(1)} custom-call(bf16[384,4096]{1,0:T(8,128)(2,1)S(1)} %copy-done, bf16[8,6144]{1,0:T(8,128)(2,1)S(1)} %collective-permute-done.rest_0_, bf16[8,6144]{1,0:T(8,128)(2,1)S(1)} %collective-permute-done.2.rest_1_, bf16[16,6144]{1,0:T(8,128)(2,1)S(1)} %collective-permute-done.4.rest_2_, ...), custom_call_target="tpu_custom_call" | custom-call | flops 1000000000 | bytes 4194304 | tf_op jit(solution)/shard_map/late/pallas_call | solution.py:143
  19.5 0.5 %collective-permute-done.6.got = f32[200,128]{1,0:T(8,128)S(1)} collective-permute-done((f32[200,128]{1,0:T(8,128)S(1)}, f32[200,128]{1,0:T(8,128)S(1)}, u32[]{:S(2)}, u32[]{:S(2)}) %collective-permute-start.6) | collective-permute-done | bytes 102432 | tf_op jit(solution)/shard_map/ppermute | solution.py:211
  20.0 0.7 %finish.1 = f32[192,96]{1,0:T(8,128)} custom-call(f32[200,128]{1,0:T(8,128)S(1)} %late.2.keep, f32[200,128]{1,0:T(8,128)S(1)} %collective-permute-done.6.got), custom_call_target="tpu_custom_call" | custom-call | flops 1000000000 | bytes 4194304 | tf_op jit(solution)/shard_map/finish/pallas_call | solution.py:143
  (1 shorter events, 0.0 us)
Async XLA Ops:
  0.0 8.3 %copy-start = (bf16[384,4096]{1,0:T(8,128)(2,1)S(1)}, bf16[384,4096]{1,0:T(8,128)(2,1)}, u32[]{:S(2)}) copy-start(bf16[384,4096]{1,0:T(8,128)(2,1)} %documents.7) | copy-start | bytes 9437188
  1.1 9.2 %collective-permute-start.1 = (bf16[8,6144]{1,0:T(8,128)(2,1)S(1)}, bf16[8,6144]{1,0:T(8,128)(2,1)S(1)}, u32[]{:S(2)}, u32[]{:S(2)}) collective-permute-start(bf16[8,6144]{1,0:T(8,128)(2,1)S(1)} %pack.1.rest_0_), channel_id=1, source_target_pairs={{0,8},{2,10},{4,12},{6,14},{8,0},{10,2},{12,4},{14,6},{1,9},{3,11}... | collective-permute-start | bytes 294920 | tf_op jit(solution)/shard_map/ppermute | solution.py:175
  5.2 6.3 %collective-permute-start.3 = (bf16[8,6144]{1,0:T(8,128)(2,1)S(1)}, bf16[8,6144]{1,0:T(8,128)(2,1)S(1)}, u32[]{:S(2)}, u32[]{:S(2)}) collective-permute-start(bf16[8,6144]{1,0:T(8,128)(2,1)S(1)} %pack.1.rest_0_), channel_id=1, source_target_pairs={{0,4},{2,6},{4,0},{6,2},{8,12},{10,14},{12,8},{14,10},{1,3},{3,1},... | collective-permute-start | bytes 294920 | tf_op jit(solution)/shard_map/ppermute | solution.py:176
  6.8 6.1 %collective-permute-start.5 = (bf16[8,6144]{1,0:T(8,128)(2,1)S(1)}, bf16[8,6144]{1,0:T(8,128)(2,1)S(1)}, u32[]{:S(2)}, u32[]{:S(2)}) collective-permute-start(bf16[8,6144]{1,0:T(8,128)(2,1)S(1)} %pack.1.rest_0_), channel_id=1, source_target_pairs={{0,2},{2,0},{4,6},{6,4},{8,10},{10,8},{12,14},{14,12},{1,5},{3,7},... | collective-permute-start | bytes 294920 | tf_op jit(solution)/shard_map/ppermute | solution.py:177
  8.3 7.5 %collective-permute-start = (bf16[8,6144]{1,0:T(8,128)(2,1)S(1)}, bf16[8,6144]{1,0:T(8,128)(2,1)S(1)}, u32[]{:S(2)}, u32[]{:S(2)}) collective-permute-start(bf16[8,6144]{1,0:T(8,128)(2,1)S(1)} %pack.1.rest_0_), channel_id=1, source_target_pairs={{0,14},{2,12},{4,10},{6,8},{8,6},{10,4},{12,2},{14,0},{1,15},{3,13... | collective-permute-start | bytes 294920 | tf_op jit(solution)/shard_map/ppermute | solution.py:178
  10.3 6.5 %collective-permute-start.2 = (bf16[8,6144]{1,0:T(8,128)(2,1)S(1)}, bf16[8,6144]{1,0:T(8,128)(2,1)S(1)}, u32[]{:S(2)}, u32[]{:S(2)}) collective-permute-start(bf16[8,6144]{1,0:T(8,128)(2,1)S(1)} %collective-permute-done.1.second), channel_id=1, source_target_pairs={{0,4},{2,6},{4,0},{6,2},{8,12},{10,14},{12,8},{14,10},{1,3},{3,1},... | collective-permute-start | bytes 294920 | tf_op jit(solution)/shard_map/ppermute | solution.py:181
  11.6 6.3 %collective-permute-start.4 = (bf16[16,6144]{1,0:T(8,128)(2,1)S(1)}, bf16[16,6144]{1,0:T(8,128)(2,1)S(1)}, u32[]{:S(2)}, u32[]{:S(2)}) collective-permute-start(bf16[16,6144]{1,0:T(8,128)(2,1)S(1)} %join.1.rest_2_), channel_id=1, source_target_pairs={{0,2},{2,0},{4,6},{6,4},{8,10},{10,8},{12,14},{14,12},{1,5},{3,7},... | collective-permute-start | bytes 589832 | tf_op jit(solution)/shard_map/ppermute | solution.py:183
  18.6 1.4 %collective-permute-start.6 = (f32[200,128]{1,0:T(8,128)S(1)}, f32[200,128]{1,0:T(8,128)S(1)}, u32[]{:S(2)}, u32[]{:S(2)}) collective-permute-start(f32[200,128]{1,0:T(8,128)S(1)} %late.3), channel_id=1, source_target_pairs={{0,1},{1,0},{2,3},{3,2},{4,5},{5,4},{6,7},{7,6},{8,9},{9,8},{10,11... | collective-permute-start | bytes 307208 | tf_op jit(solution)/shard_map/ppermute | solution.py:211

commit v5 on v4

--- a/solution.py
+++ b/solution.py
@@ -129,16 +129,6 @@
     scores[...] = (total[:half] * doc_scale * query_scale)[:, :width]
 
 
-def squared_paths(blocks):
-    one = [(b, b ^ 1) for b in range(blocks)]
-    two = [(b, b ^ 2) for b in range(blocks)]
-    far = [(b, b ^ 4) for b in range(blocks)]
-    first = [(2 * b, 2 * c) for b, c in two] + [(2 * b + 1, 2 * c + 1) for b, c in one]
-    second = [(2 * b, 2 * c) for b, c in one] + [(2 * b + 1, 2 * c + 1) for b, c in two]
-    farthest = [(b, b ^ 7) for b in range(blocks)]
-    return far, farthest, first, second
-
-
 def call(kernel, name, out, *args, hbm=False, scratch=(), limit=24):
     return pl.pallas_call(
         kernel,
@@ -157,7 +147,11 @@
     blocks = lax.axis_size("blk")
     half = docs // 2
     lanes = 16 * blocks
-    far, farthest, first, second = squared_paths(blocks)
+
+    def by_core(even, odd):
+        steps = (even, odd)
+        return [(2 * b + c, 2 * (b ^ steps[c]) + c) for b in range(blocks) for c in range(2)]
+
     packed = call(
         pack_kernel,
         "pack",
@@ -172,36 +166,28 @@
             pltpu.SemaphoreType.DMA((2,)),
         ],
     )
-    across = lax.ppermute(packed, "blk", far)
-    n1 = lax.ppermute(packed, BOTH, first)
-    n2 = lax.ppermute(packed, BOTH, second)
-    corner = lax.ppermute(packed, "blk", farthest)
+    across = lax.ppermute(packed, BOTH, by_core(4, 4))
+    n1 = lax.ppermute(packed, BOTH, by_core(1, 2))
+    n2 = lax.ppermute(packed, BOTH, by_core(2, 1))
+    corner = lax.ppermute(packed, BOTH, by_core(7, 7))
     squares = call(squares_kernel, "squares", pltpu.VMEM((docs, 1), jnp.float32), documents)
     across, squares = lax.optimization_barrier((across, squares))
-    a1 = lax.ppermute(across, BOTH, first)
     two = call(join_kernel, "join", pltpu.VMEM((16, 3 * width // 2), jnp.bfloat16), n1, across)
-    pair = lax.ppermute(two, BOTH, second)
+    two, across = lax.optimization_barrier((two, across))
+    pair = lax.ppermute(two, BOTH, by_core(2, 1))
+    a1 = lax.ppermute(across, BOTH, by_core(1, 2))
     whole = pltpu.VMEM((lanes, width), jnp.bfloat16)
+    both = (pltpu.VMEM((docs, lanes), jnp.float32), pltpu.VMEM((8, lanes), jnp.float32))
     scores, query_squares = call(
-        functools.partial(early_kernel, (0, (1, 2), (2, 1), 4)),
-        "early",
-        (pltpu.VMEM((docs, lanes), jnp.float32), pltpu.VMEM((8, lanes), jnp.float32)),
-        documents,
-        squares,
-        packed,
-        n2,
-        two,
-        scratch=[whole],
+        functools.partial(early_kernel, (0, (1, 2), 4)), "early", both, documents, squares, packed, two, scratch=[whole]
     )
     send, keep = (
         call(
-            functools.partial(late_kernel, (7, (6, 5), 3, (5, 6)), other),
+            functools.partial(late_kernel, ((2, 1), 7, (5, 6), 3, (6, 5)), other),
             "late",
             pltpu.VMEM((half + 8, lanes), jnp.float32),
             documents,
-            corner,
-            a1,
-            pair,
+            n2, corner, a1, pair,
             scores,
             query_squares,
             scratch=[whole],

time: 20.9 us -> 20.7 us (level)
  waiting for transfers between devices: 6.16 us -> 4.71 us
  starting transfers between devices: 9.24 us -> 10.5 us
    ppermute x6, waiting for transfers between devices: 5.63 us -> 4.22 us  [the longest x1 1.21 us: by_squares(): across = lax.ppermute(packed, BOTH, by_core(4, 4))]
    ppermute x6, starting transfers between devices: 9.17 us -> 10.4 us  [the longest x1 4.1 us: by_squares(): across = lax.ppermute(packed, BOTH, by_core(4, 4))]
where the time goes in v5:
time: 20.7 us; the launch traced here: 20.6 us
  starting transfers between devices  10.5 us (51%)
  Pallas kernels  5.31 us (26%)
  waiting for transfers between devices  4.71 us (23%)
    pallas_call x7, Pallas kernels, call(): pl.pallas_call(kernel, out_shape=out, in_specs=[anywhere() if hbm else vm...  5.31 us
    ppermute x1, starting transfers between devices, by_squares(): across = lax.ppermute(packed, BOTH, by_core(4, 4))  4.1 us
    ppermute x1, starting transfers between devices, by_squares(): a1 = lax.ppermute(across, BOTH, by_core(1, 2))  1.94 us
    ppermute x1, starting transfers between devices, by_squares(): n2 = lax.ppermute(packed, BOTH, by_core(2, 1))  1.58 us
    ppermute x1, starting transfers between devices, by_squares(): n1 = lax.ppermute(packed, BOTH, by_core(1, 2))  1.49 us
    ppermute x1, starting transfers between devices, by_squares(): pair = lax.ppermute(two, BOTH, by_core(2, 1))  1.33 us
    ppermute x1, waiting for transfers between devices, by_squares(): across = lax.ppermute(packed, BOTH, by_core(4, 4))  1.21 us
    ppermute x1, waiting for transfers between devices, by_squares(): a1 = lax.ppermute(across, BOTH, by_core(1, 2))  1.05 us
  transfers between devices with their start and end apart: 7, of which 6 were waited for; matrix products, arithmetic and copies ran while one was open for 0% of the time, Pallas kernels for 13%

profile of v5, /device:TPU:0, one launch (start us, length us, event | category | flops | bytes accessed | tf_op | source)
XLA Modules:
  0.0 20.6 jit_solution(8602048684280722234)
XLA Ops:
  0.0 0.0 copy-start
  0.0 1.1 %pack.1.rest_0_ = bf16[8,6144]{1,0:T(8,128)(2,1)S(1)} custom-call(bf16[12,4096]{1,0:T(8,128)(2,1)} %queries_hbm.1, f32[1,4096]{1,0:T(1,128)} %bitcast.1), custom_call_target="tpu_custom_call" | custom-call | flops 1000000000 | bytes 4194304 | tf_op jit(solution)/shard_map/pack/pallas_call | solution.py:133
  1.1 4.1 %collective-permute-start.3 = (bf16[8,6144]{1,0:T(8,128)(2,1)S(1)}, bf16[8,6144]{1,0:T(8,128)(2,1)S(1)}, u32[]{:S(2)}, u32[]{:S(2)}) collective-permute-start(bf16[8,6144]{1,0:T(8,128)(2,1)S(1)} %pack.1.rest_0_), channel_id=1, source_target_pairs={{0,8},{1,9},{2,10},{3,11},{4,12},{5,13},{6,14},{7,15},{8,0},{9,1},... | collective-permute-start | bytes 294920 | tf_op jit(solution)/shard_map/ppermute | solution.py:169
  5.2 1.5 %collective-permute-start.2 = (bf16[8,6144]{1,0:T(8,128)(2,1)S(1)}, bf16[8,6144]{1,0:T(8,128)(2,1)S(1)}, u32[]{:S(2)}, u32[]{:S(2)}) collective-permute-start(bf16[8,6144]{1,0:T(8,128)(2,1)S(1)} %pack.1.rest_0_), channel_id=1, source_target_pairs={{0,2},{1,5},{2,0},{3,7},{4,6},{5,1},{6,4},{7,3},{8,10},{9,13},{10,... | collective-permute-start | bytes 294920 | tf_op jit(solution)/shard_map/ppermute | solution.py:170
  6.7 1.6 %collective-permute-start = (bf16[8,6144]{1,0:T(8,128)(2,1)S(1)}, bf16[8,6144]{1,0:T(8,128)(2,1)S(1)}, u32[]{:S(2)}, u32[]{:S(2)}) collective-permute-start(bf16[8,6144]{1,0:T(8,128)(2,1)S(1)} %pack.1.rest_0_), channel_id=1, source_target_pairs={{0,4},{1,3},{2,6},{3,1},{4,0},{5,7},{6,2},{7,5},{8,12},{9,11},{10,... | collective-permute-start | bytes 294920 | tf_op jit(solution)/shard_map/ppermute | solution.py:171
  8.3 0.0 collective-permute-start.1
  8.3 0.0 copy-done
  8.3 0.7 %squares.1 = f32[384,1]{1,0:T(8,128)S(1)} custom-call(bf16[384,4096]{1,0:T(8,128)(2,1)S(1)} %copy-done), custom_call_target="tpu_custom_call" | custom-call | flops 20000000000 | bytes 4194304 | tf_op jit(solution)/shard_map/squares/pallas_call | solution.py:133
  9.0 1.2 %collective-permute-done.3.second = bf16[8,6144]{1,0:T(8,128)(2,1)S(1)} collective-permute-done((bf16[8,6144]{1,0:T(8,128)(2,1)S(1)}, bf16[8,6144]{1,0:T(8,128)(2,1)S(1)}, u32[]{:S(2)}, u32[]{:S(2)}) %collective-permute-start.3) | collective-permute-done | bytes 98336 | tf_op jit(solution)/shard_map/ppermute | solution.py:169
  10.2 0.6 %collective-permute-done.2.first = bf16[8,6144]{1,0:T(8,128)(2,1)S(1)} collective-permute-done((bf16[8,6144]{1,0:T(8,128)(2,1)S(1)}, bf16[8,6144]{1,0:T(8,128)(2,1)S(1)}, u32[]{:S(2)}, u32[]{:S(2)}) %collective-permute-start.2) | collective-permute-done | bytes 98336 | tf_op jit(solution)/shard_map/ppermute | solution.py:170
  10.8 1.3 %collective-permute-start.5 = (bf16[16,6144]{1,0:T(8,128)(2,1)S(1)}, bf16[16,6144]{1,0:T(8,128)(2,1)S(1)}, u32[]{:S(2)}, u32[]{:S(2)}) collective-permute-start(bf16[16,6144]{1,0:T(8,128)(2,1)S(1)} %join.1.rest_1_), channel_id=1, source_target_pairs={{0,4},{1,3},{2,6},{3,1},{4,0},{5,7},{6,2},{7,5},{8,12},{9,11},{10,... | collective-permute-start | bytes 589832 | tf_op jit(solution)/shard_map/ppermute | solution.py:177
  12.1 1.9 %collective-permute-start.4 = (bf16[8,6144]{1,0:T(8,128)(2,1)S(1)}, bf16[8,6144]{1,0:T(8,128)(2,1)S(1)}, u32[]{:S(2)}, u32[]{:S(2)}) collective-permute-start(bf16[8,6144]{1,0:T(8,128)(2,1)S(1)} %collective-permute-done.3.second), channel_id=1, source_target_pairs={{0,2},{1,5},{2,0},{3,7},{4,6},{5,1},{6,4},{7,3},{8,10},{9,13},{10,... | collective-permute-start | bytes 294920 | tf_op jit(solution)/shard_map/ppermute | solution.py:178
  14.1 1.2 %early.1 = (f32[384,128]{1,0:T(8,128)S(1)}, f32[8,128]{1,0:T(8,128)S(1)}) custom-call(bf16[384,4096]{1,0:T(8,128)(2,1)S(1)} %copy-done, f32[384,1]{1,0:T(8,128)S(1)} %squares.1, bf16[8,6144]{1,0:T(8,128)(2,1)S(1)} %pack.1.rest_0_, bf16[16,6144]{1,0:T(8,128)(2,1)S(1)} %join.1.rest_1_), custom_call_target="tpu_custom_call" | custom-call | flops 20000000000 | bytes 4194304 | tf_op jit(solution)/shard_map/early/pallas_call | solution.py:133
  15.2 0.0 collective-permute-done.rest_0_
  15.3 0.5 %collective-permute-done.1.rest_1_ = bf16[8,6144]{1,0:T(8,128)(2,1)S(1)} collective-permute-done((bf16[8,6144]{1,0:T(8,128)(2,1)S(1)}, bf16[8,6144]{1,0:T(8,128)(2,1)S(1)}, u32[]{:S(2)}, u32[]{:S(2)}) %collective-permute-start.1) | collective-permute-done | bytes 98336 | tf_op jit(solution)/shard_map/ppermute | solution.py:172
  15.8 1.0 %collective-permute-done.4.rest_2_ = bf16[8,6144]{1,0:T(8,128)(2,1)S(1)} collective-permute-done((bf16[8,6144]{1,0:T(8,128)(2,1)S(1)}, bf16[8,6144]{1,0:T(8,128)(2,1)S(1)}, u32[]{:S(2)}, u32[]{:S(2)}) %collective-permute-start.4) | collective-permute-done | bytes 98336 | tf_op jit(solution)/shard_map/ppermute | solution.py:178
  16.8 0.9 %collective-permute-done.5.rest_3_ = bf16[16,6144]{1,0:T(8,128)(2,1)S(1)} collective-permute-done((bf16[16,6144]{1,0:T(8,128)(2,1)S(1)}, bf16[16,6144]{1,0:T(8,128)(2,1)S(1)}, u32[]{:S(2)}, u32[]{:S(2)}) %collective-permute-start.5) | collective-permute-done | bytes 196640 | tf_op jit(solution)/shard_map/ppermute | solution.py:177
  17.7 0.8 %late.3 = f32[200,128]{1,0:T(8,128)S(1)} custom-call(bf16[384,4096]{1,0:T(8,128)(2,1)S(1)} %copy-done, bf16[8,6144]{1,0:T(8,128)(2,1)S(1)} %collective-permute-done.rest_0_, bf16[8,6144]{1,0:T(8,128)(2,1)S(1)} %collective-permute-done.1.rest_1_, bf16[8,6144]{1,0:T(8,128)(2,1)S(1)} %collective-permute-done.4.rest_2_, ...), custom_call_target="tpu_custom_call" | custom-call | flops 1000000000 | bytes 4194304 | tf_op jit(solution)/shard_map/late/pallas_call | solution.py:133
  18.5 0.1 collective-permute-start.6
  18.6 0.8 %late.2.keep = f32[200,128]{1,0:T(8,128)S(1)} custom-call(bf16[384,4096]{1,0:T(8,128)(2,1)S(1)} %copy-done, bf16[8,6144]{1,0:T(8,128)(2,1)S(1)} %collective-permute-done.rest_0_, bf16[8,6144]{1,0:T(8,128)(2,1)S(1)} %collective-permute-done.1.rest_1_, bf16[8,6144]{1,0:T(8,128)(2,1)S(1)} %collective-permute-done.4.rest_2_, ...), custom_call_target="tpu_custom_call" | custom-call | flops 1000000000 | bytes 4194304 | tf_op jit(solution)/shard_map/late/pallas_call | solution.py:133
  19.4 0.5 %collective-permute-done.6.got = f32[200,128]{1,0:T(8,128)S(1)} collective-permute-done((f32[200,128]{1,0:T(8,128)S(1)}, f32[200,128]{1,0:T(8,128)S(1)}, u32[]{:S(2)}, u32[]{:S(2)}) %collective-permute-start.6) | collective-permute-done | bytes 102432 | tf_op jit(solution)/shard_map/ppermute | solution.py:197
  19.9 0.7 %finish.1 = f32[192,96]{1,0:T(8,128)} custom-call(f32[200,128]{1,0:T(8,128)S(1)} %late.2.keep, f32[200,128]{1,0:T(8,128)S(1)} %collective-permute-done.6.got), custom_call_target="tpu_custom_call" | custom-call | flops 1000000000 | bytes 4194304 | tf_op jit(solution)/shard_map/finish/pallas_call | solution.py:133
  (1 shorter events, 0.0 us)
Async XLA Ops:
  0.0 8.3 %copy-start = (bf16[384,4096]{1,0:T(8,128)(2,1)S(1)}, bf16[384,4096]{1,0:T(8,128)(2,1)}, u32[]{:S(2)}) copy-start(bf16[384,4096]{1,0:T(8,128)(2,1)} %documents.7) | copy-start | bytes 9437188
  1.1 9.1 %collective-permute-start.3 = (bf16[8,6144]{1,0:T(8,128)(2,1)S(1)}, bf16[8,6144]{1,0:T(8,128)(2,1)S(1)}, u32[]{:S(2)}, u32[]{:S(2)}) collective-permute-start(bf16[8,6144]{1,0:T(8,128)(2,1)S(1)} %pack.1.rest_0_), channel_id=1, source_target_pairs={{0,8},{1,9},{2,10},{3,11},{4,12},{5,13},{6,14},{7,15},{8,0},{9,1},... | collective-permute-start | bytes 294920 | tf_op jit(solution)/shard_map/ppermute | solution.py:169
  5.2 5.6 %collective-permute-start.2 = (bf16[8,6144]{1,0:T(8,128)(2,1)S(1)}, bf16[8,6144]{1,0:T(8,128)(2,1)S(1)}, u32[]{:S(2)}, u32[]{:S(2)}) collective-permute-start(bf16[8,6144]{1,0:T(8,128)(2,1)S(1)} %pack.1.rest_0_), channel_id=1, source_target_pairs={{0,2},{1,5},{2,0},{3,7},{4,6},{5,1},{6,4},{7,3},{8,10},{9,13},{10,... | collective-permute-start | bytes 294920 | tf_op jit(solution)/shard_map/ppermute | solution.py:170
  6.7 8.5 %collective-permute-start = (bf16[8,6144]{1,0:T(8,128)(2,1)S(1)}, bf16[8,6144]{1,0:T(8,128)(2,1)S(1)}, u32[]{:S(2)}, u32[]{:S(2)}) collective-permute-start(bf16[8,6144]{1,0:T(8,128)(2,1)S(1)} %pack.1.rest_0_), channel_id=1, source_target_pairs={{0,4},{1,3},{2,6},{3,1},{4,0},{5,7},{6,2},{7,5},{8,12},{9,11},{10,... | collective-permute-start | bytes 294920 | tf_op jit(solution)/shard_map/ppermute | solution.py:171
  8.3 7.5 %collective-permute-start.1 = (bf16[8,6144]{1,0:T(8,128)(2,1)S(1)}, bf16[8,6144]{1,0:T(8,128)(2,1)S(1)}, u32[]{:S(2)}, u32[]{:S(2)}) collective-permute-start(bf16[8,6144]{1,0:T(8,128)(2,1)S(1)} %pack.1.rest_0_), channel_id=1, source_target_pairs={{0,14},{1,15},{2,12},{3,13},{4,10},{5,11},{6,8},{7,9},{8,6},{9,7},... | collective-permute-start | bytes 294920 | tf_op jit(solution)/shard_map/ppermute | solution.py:172
  10.8 6.9 %collective-permute-start.5 = (bf16[16,6144]{1,0:T(8,128)(2,1)S(1)}, bf16[16,6144]{1,0:T(8,128)(2,1)S(1)}, u32[]{:S(2)}, u32[]{:S(2)}) collective-permute-start(bf16[16,6144]{1,0:T(8,128)(2,1)S(1)} %join.1.rest_1_), channel_id=1, source_target_pairs={{0,4},{1,3},{2,6},{3,1},{4,0},{5,7},{6,2},{7,5},{8,12},{9,11},{10,... | collective-permute-start | bytes 589832 | tf_op jit(solution)/shard_map/ppermute | solution.py:177
  12.1 4.7 %collective-permute-start.4 = (bf16[8,6144]{1,0:T(8,128)(2,1)S(1)}, bf16[8,6144]{1,0:T(8,128)(2,1)S(1)}, u32[]{:S(2)}, u32[]{:S(2)}) collective-permute-start(bf16[8,6144]{1,0:T(8,128)(2,1)S(1)} %collective-permute-done.3.second), channel_id=1, source_target_pairs={{0,2},{1,5},{2,0},{3,7},{4,6},{5,1},{6,4},{7,3},{8,10},{9,13},{10,... | collective-permute-start | bytes 294920 | tf_op jit(solution)/shard_map/ppermute | solution.py:178
  18.5 1.4 %collective-permute-start.6 = (f32[200,128]{1,0:T(8,128)S(1)}, f32[200,128]{1,0:T(8,128)S(1)}, u32[]{:S(2)}, u32[]{:S(2)}) collective-permute-start(f32[200,128]{1,0:T(8,128)S(1)} %late.3), channel_id=1, source_target_pairs={{0,1},{1,0},{2,3},{3,2},{4,5},{5,4},{6,7},{7,6},{8,9},{9,8},{10,11... | collective-permute-start | bytes 307208 | tf_op jit(solution)/shard_map/ppermute | solution.py:197

commit v6 on v5

--- a/solution.py
+++ b/solution.py
@@ -166,24 +166,23 @@
             pltpu.SemaphoreType.DMA((2,)),
         ],
     )
-    across = lax.ppermute(packed, BOTH, by_core(4, 4))
-    n1 = lax.ppermute(packed, BOTH, by_core(1, 2))
-    n2 = lax.ppermute(packed, BOTH, by_core(2, 1))
-    corner = lax.ppermute(packed, BOTH, by_core(7, 7))
+    across = lax.ppermute(packed, BOTH, by_core(6, 4))
+    n1 = lax.ppermute(packed, BOTH, by_core(2, 1))
+    n2 = lax.ppermute(packed, BOTH, by_core(1, 2))
+    corner = lax.ppermute(packed, BOTH, by_core(5, 7))
     squares = call(squares_kernel, "squares", pltpu.VMEM((docs, 1), jnp.float32), documents)
     across, squares = lax.optimization_barrier((across, squares))
+    a1 = lax.ppermute(across, BOTH, by_core(2, 1))
     two = call(join_kernel, "join", pltpu.VMEM((16, 3 * width // 2), jnp.bfloat16), n1, across)
-    two, across = lax.optimization_barrier((two, across))
-    pair = lax.ppermute(two, BOTH, by_core(2, 1))
-    a1 = lax.ppermute(across, BOTH, by_core(1, 2))
+    pair = lax.ppermute(two, BOTH, by_core(1, 2))
     whole = pltpu.VMEM((lanes, width), jnp.bfloat16)
     both = (pltpu.VMEM((docs, lanes), jnp.float32), pltpu.VMEM((8, lanes), jnp.float32))
     scores, query_squares = call(
-        functools.partial(early_kernel, (0, (1, 2), 4)), "early", both, documents, squares, packed, two, scratch=[whole]
+        functools.partial(early_kernel, (0, (2, 1), (6, 4))), "early", both, documents, squares, packed, two, scratch=[whole]
     )
     send, keep = (
         call(
-            functools.partial(late_kernel, ((2, 1), 7, (5, 6), 3, (6, 5)), other),
+            functools.partial(late_kernel, ((1, 2), (5, 7), (4, 5), 3, (7, 6)), other),
             "late",
             pltpu.VMEM((half + 8, lanes), jnp.float32),
             documents,

time: 20.7 us -> 20.1 us (0.971)
  waiting for transfers between devices: 4.71 us -> 4.19 us
    ppermute x6, waiting for transfers between devices: 4.22 us -> 3.7 us  [the longest x1 1.27 us: by_squares(): corner = lax.ppermute(packed, BOTH, by_core(5, 7))]
  transfers between devices with their start and end apart: 7 -> 7, of which waited for: 6 -> 5; matrix products, arithmetic and copies ran while one was open for 0% -> 0% of each run, Pallas kernels for 13% -> 13%
where the time goes in v6:
time: 20.1 us; the launch traced here: 20 us
  starting transfers between devices  10.4 us (52%)
  Pallas kernels  5.3 us (26%)
  waiting for transfers between devices  4.19 us (21%)
    pallas_call x7, Pallas kernels, call(): pl.pallas_call(kernel, out_shape=out, in_specs=[anywhere() if hbm else vm...  5.3 us
    ppermute x1, starting transfers between devices, by_squares(): across = lax.ppermute(packed, BOTH, by_core(6, 4))  5.11 us
    ppermute x1, starting transfers between devices, by_squares(): pair = lax.ppermute(two, BOTH, by_core(1, 2))  2.03 us
    ppermute x1, starting transfers between devices, by_squares(): n2 = lax.ppermute(packed, BOTH, by_core(1, 2))  1.49 us
    ppermute x1, waiting for transfers between devices, by_squares(): corner = lax.ppermute(packed, BOTH, by_core(5, 7))  1.27 us
    ppermute x1, waiting for transfers between devices, by_squares(): pair = lax.ppermute(two, BOTH, by_core(1, 2))  1.22 us
    ppermute x1, starting transfers between devices, by_squares(): a1 = lax.ppermute(across, BOTH, by_core(2, 1))  1.13 us
    ppermute x1, waiting for transfers between devices, by_squares(): across = lax.ppermute(packed, BOTH, by_core(6, 4))  0.81 us
  transfers between devices with their start and end apart: 7, of which 5 were waited for; matrix products, arithmetic and copies ran while one was open for 0% of the time, Pallas kernels for 13%

profile of v6, /device:TPU:0, one launch (start us, length us, event | category | flops | bytes accessed | tf_op | source)
XLA Modules:
  0.0 20.0 jit_solution(12623791606084104710)
XLA Ops:
  0.0 0.0 copy-start
  0.0 1.1 %pack.1.rest_0_ = bf16[8,6144]{1,0:T(8,128)(2,1)S(1)} custom-call(bf16[12,4096]{1,0:T(8,128)(2,1)} %queries_hbm.1, f32[1,4096]{1,0:T(1,128)} %bitcast.1), custom_call_target="tpu_custom_call" | custom-call | flops 1000000000 | bytes 4194304 | tf_op jit(solution)/shard_map/pack/pallas_call | solution.py:133
  1.1 5.1 %collective-permute-start.2 = (bf16[8,6144]{1,0:T(8,128)(2,1)S(1)}, bf16[8,6144]{1,0:T(8,128)(2,1)S(1)}, u32[]{:S(2)}, u32[]{:S(2)}) collective-permute-start(bf16[8,6144]{1,0:T(8,128)(2,1)S(1)} %pack.1.rest_0_), channel_id=1, source_target_pairs={{0,12},{1,9},{2,14},{3,11},{4,8},{5,13},{6,10},{7,15},{8,4},{9,1},... | collective-permute-start | bytes 294920 | tf_op jit(solution)/shard_map/ppermute | solution.py:169
  6.2 0.0 collective-permute-start.4
  6.2 1.5 %collective-permute-start = (bf16[8,6144]{1,0:T(8,128)(2,1)S(1)}, bf16[8,6144]{1,0:T(8,128)(2,1)S(1)}, u32[]{:S(2)}, u32[]{:S(2)}) collective-permute-start(bf16[8,6144]{1,0:T(8,128)(2,1)S(1)} %pack.1.rest_0_), channel_id=1, source_target_pairs={{0,2},{1,5},{2,0},{3,7},{4,6},{5,1},{6,4},{7,3},{8,10},{9,13},{10,... | collective-permute-start | bytes 294920 | tf_op jit(solution)/shard_map/ppermute | solution.py:171
  7.7 0.6 %collective-permute-start.1 = (bf16[8,6144]{1,0:T(8,128)(2,1)S(1)}, bf16[8,6144]{1,0:T(8,128)(2,1)S(1)}, u32[]{:S(2)}, u32[]{:S(2)}) collective-permute-start(bf16[8,6144]{1,0:T(8,128)(2,1)S(1)} %pack.1.rest_0_), channel_id=1, source_target_pairs={{0,10},{1,15},{2,8},{3,13},{4,14},{5,11},{6,12},{7,9},{8,2},{9,7},... | collective-permute-start | bytes 294920 | tf_op jit(solution)/shard_map/ppermute | solution.py:172
  8.3 0.0 copy-done
  8.3 0.7 %squares.1 = f32[384,1]{1,0:T(8,128)S(1)} custom-call(bf16[384,4096]{1,0:T(8,128)(2,1)S(1)} %copy-done), custom_call_target="tpu_custom_call" | custom-call | flops 20000000000 | bytes 4194304 | tf_op jit(solution)/shard_map/squares/pallas_call | solution.py:133
  9.0 0.8 %collective-permute-done.2.second = bf16[8,6144]{1,0:T(8,128)(2,1)S(1)} collective-permute-done((bf16[8,6144]{1,0:T(8,128)(2,1)S(1)}, bf16[8,6144]{1,0:T(8,128)(2,1)S(1)}, u32[]{:S(2)}, u32[]{:S(2)}) %collective-permute-start.2) | collective-permute-done | bytes 98336 | tf_op jit(solution)/shard_map/ppermute | solution.py:169
  9.8 1.1 %collective-permute-start.3 = (bf16[8,6144]{1,0:T(8,128)(2,1)S(1)}, bf16[8,6144]{1,0:T(8,128)(2,1)S(1)}, u32[]{:S(2)}, u32[]{:S(2)}) collective-permute-start(bf16[8,6144]{1,0:T(8,128)(2,1)S(1)} %collective-permute-done.2.second), channel_id=1, source_target_pairs={{0,4},{1,3},{2,6},{3,1},{4,0},{5,7},{6,2},{7,5},{8,12},{9,11},{10,... | collective-permute-start | bytes 294920 | tf_op jit(solution)/shard_map/ppermute | solution.py:175
  11.0 0.3 %collective-permute-done.4.first = bf16[8,6144]{1,0:T(8,128)(2,1)S(1)} collective-permute-done((bf16[8,6144]{1,0:T(8,128)(2,1)S(1)}, bf16[8,6144]{1,0:T(8,128)(2,1)S(1)}, u32[]{:S(2)}, u32[]{:S(2)}) %collective-permute-start.4) | collective-permute-done | bytes 98336 | tf_op jit(solution)/shard_map/ppermute | solution.py:170
  11.3 2.0 %collective-permute-start.5 = (bf16[16,6144]{1,0:T(8,128)(2,1)S(1)}, bf16[16,6144]{1,0:T(8,128)(2,1)S(1)}, u32[]{:S(2)}, u32[]{:S(2)}) collective-permute-start(bf16[16,6144]{1,0:T(8,128)(2,1)S(1)} %join.1.rest_1_), channel_id=1, source_target_pairs={{0,2},{1,5},{2,0},{3,7},{4,6},{5,1},{6,4},{7,3},{8,10},{9,13},{10,... | collective-permute-start | bytes 589832 | tf_op jit(solution)/shard_map/ppermute | solution.py:177
  13.4 1.2 %early.1 = (f32[384,128]{1,0:T(8,128)S(1)}, f32[8,128]{1,0:T(8,128)S(1)}) custom-call(bf16[384,4096]{1,0:T(8,128)(2,1)S(1)} %copy-done, f32[384,1]{1,0:T(8,128)S(1)} %squares.1, bf16[8,6144]{1,0:T(8,128)(2,1)S(1)} %pack.1.rest_0_, bf16[16,6144]{1,0:T(8,128)(2,1)S(1)} %join.1.rest_1_), custom_call_target="tpu_custom_call" | custom-call | flops 20000000000 | bytes 4194304 | tf_op jit(solution)/shard_map/early/pallas_call | solution.py:133
  14.5 0.0 collective-permute-done.rest_0_
  14.6 1.3 %collective-permute-done.1.rest_1_ = bf16[8,6144]{1,0:T(8,128)(2,1)S(1)} collective-permute-done((bf16[8,6144]{1,0:T(8,128)(2,1)S(1)}, bf16[8,6144]{1,0:T(8,128)(2,1)S(1)}, u32[]{:S(2)}, u32[]{:S(2)}) %collective-permute-start.1) | collective-permute-done | bytes 98336 | tf_op jit(solution)/shard_map/ppermute | solution.py:172
  15.8 0.0 collective-permute-done.3.rest_2_
  15.9 1.2 %collective-permute-done.5.rest_3_ = bf16[16,6144]{1,0:T(8,128)(2,1)S(1)} collective-permute-done((bf16[16,6144]{1,0:T(8,128)(2,1)S(1)}, bf16[16,6144]{1,0:T(8,128)(2,1)S(1)}, u32[]{:S(2)}, u32[]{:S(2)}) %collective-permute-start.5) | collective-permute-done | bytes 196640 | tf_op jit(solution)/shard_map/ppermute | solution.py:177
  17.1 0.8 %late.3 = f32[200,128]{1,0:T(8,128)S(1)} custom-call(bf16[384,4096]{1,0:T(8,128)(2,1)S(1)} %copy-done, bf16[8,6144]{1,0:T(8,128)(2,1)S(1)} %collective-permute-done.rest_0_, bf16[8,6144]{1,0:T(8,128)(2,1)S(1)} %collective-permute-done.1.rest_1_, bf16[8,6144]{1,0:T(8,128)(2,1)S(1)} %collective-permute-done.3.rest_2_, ...), custom_call_target="tpu_custom_call" | custom-call | flops 1000000000 | bytes 4194304 | tf_op jit(solution)/shard_map/late/pallas_call | solution.py:133
  17.9 0.1 collective-permute-start.6
  18.0 0.8 %late.2.keep = f32[200,128]{1,0:T(8,128)S(1)} custom-call(bf16[384,4096]{1,0:T(8,128)(2,1)S(1)} %copy-done, bf16[8,6144]{1,0:T(8,128)(2,1)S(1)} %collective-permute-done.rest_0_, bf16[8,6144]{1,0:T(8,128)(2,1)S(1)} %collective-permute-done.1.rest_1_, bf16[8,6144]{1,0:T(8,128)(2,1)S(1)} %collective-permute-done.3.rest_2_, ...), custom_call_target="tpu_custom_call" | custom-call | flops 1000000000 | bytes 4194304 | tf_op jit(solution)/shard_map/late/pallas_call | solution.py:133
  18.8 0.5 %collective-permute-done.6.got = f32[200,128]{1,0:T(8,128)S(1)} collective-permute-done((f32[200,128]{1,0:T(8,128)S(1)}, f32[200,128]{1,0:T(8,128)S(1)}, u32[]{:S(2)}, u32[]{:S(2)}) %collective-permute-start.6) | collective-permute-done | bytes 102432 | tf_op jit(solution)/shard_map/ppermute | solution.py:196
  19.3 0.7 %finish.1 = f32[192,96]{1,0:T(8,128)} custom-call(f32[200,128]{1,0:T(8,128)S(1)} %late.2.keep, f32[200,128]{1,0:T(8,128)S(1)} %collective-permute-done.6.got), custom_call_target="tpu_custom_call" | custom-call | flops 1000000000 | bytes 4194304 | tf_op jit(solution)/shard_map/finish/pallas_call | solution.py:133
  (1 shorter events, 0.0 us)
Async XLA Ops:
  0.0 8.3 %copy-start = (bf16[384,4096]{1,0:T(8,128)(2,1)S(1)}, bf16[384,4096]{1,0:T(8,128)(2,1)}, u32[]{:S(2)}) copy-start(bf16[384,4096]{1,0:T(8,128)(2,1)} %documents.7) | copy-start | bytes 9437188
  1.1 8.7 %collective-permute-start.2 = (bf16[8,6144]{1,0:T(8,128)(2,1)S(1)}, bf16[8,6144]{1,0:T(8,128)(2,1)S(1)}, u32[]{:S(2)}, u32[]{:S(2)}) collective-permute-start(bf16[8,6144]{1,0:T(8,128)(2,1)S(1)} %pack.1.rest_0_), channel_id=1, source_target_pairs={{0,12},{1,9},{2,14},{3,11},{4,8},{5,13},{6,10},{7,15},{8,4},{9,1},... | collective-permute-start | bytes 294920 | tf_op jit(solution)/shard_map/ppermute | solution.py:169
  6.2 5.1 %collective-permute-start.4 = (bf16[8,6144]{1,0:T(8,128)(2,1)S(1)}, bf16[8,6144]{1,0:T(8,128)(2,1)S(1)}, u32[]{:S(2)}, u32[]{:S(2)}) collective-permute-start(bf16[8,6144]{1,0:T(8,128)(2,1)S(1)} %pack.1.rest_0_), channel_id=1, source_target_pairs={{0,4},{1,3},{2,6},{3,1},{4,0},{5,7},{6,2},{7,5},{8,12},{9,11},{10,... | collective-permute-start | bytes 294920 | tf_op jit(solution)/shard_map/ppermute | solution.py:170
  6.2 8.3 %collective-permute-start = (bf16[8,6144]{1,0:T(8,128)(2,1)S(1)}, bf16[8,6144]{1,0:T(8,128)(2,1)S(1)}, u32[]{:S(2)}, u32[]{:S(2)}) collective-permute-start(bf16[8,6144]{1,0:T(8,128)(2,1)S(1)} %pack.1.rest_0_), channel_id=1, source_target_pairs={{0,2},{1,5},{2,0},{3,7},{4,6},{5,1},{6,4},{7,3},{8,10},{9,13},{10,... | collective-permute-start | bytes 294920 | tf_op jit(solution)/shard_map/ppermute | solution.py:171
  7.7 8.1 %collective-permute-start.1 = (bf16[8,6144]{1,0:T(8,128)(2,1)S(1)}, bf16[8,6144]{1,0:T(8,128)(2,1)S(1)}, u32[]{:S(2)}, u32[]{:S(2)}) collective-permute-start(bf16[8,6144]{1,0:T(8,128)(2,1)S(1)} %pack.1.rest_0_), channel_id=1, source_target_pairs={{0,10},{1,15},{2,8},{3,13},{4,14},{5,11},{6,12},{7,9},{8,2},{9,7},... | collective-permute-start | bytes 294920 | tf_op jit(solution)/shard_map/ppermute | solution.py:172
  9.8 6.0 %collective-permute-start.3 = (bf16[8,6144]{1,0:T(8,128)(2,1)S(1)}, bf16[8,6144]{1,0:T(8,128)(2,1)S(1)}, u32[]{:S(2)}, u32[]{:S(2)}) collective-permute-start(bf16[8,6144]{1,0:T(8,128)(2,1)S(1)} %collective-permute-done.2.second), channel_id=1, source_target_pairs={{0,4},{1,3},{2,6},{3,1},{4,0},{5,7},{6,2},{7,5},{8,12},{9,11},{10,... | collective-permute-start | bytes 294920 | tf_op jit(solution)/shard_map/ppermute | solution.py:175
  11.3 5.8 %collective-permute-start.5 = (bf16[16,6144]{1,0:T(8,128)(2,1)S(1)}, bf16[16,6144]{1,0:T(8,128)(2,1)S(1)}, u32[]{:S(2)}, u32[]{:S(2)}) collective-permute-start(bf16[16,6144]{1,0:T(8,128)(2,1)S(1)} %join.1.rest_1_), channel_id=1, source_target_pairs={{0,2},{1,5},{2,0},{3,7},{4,6},{5,1},{6,4},{7,3},{8,10},{9,13},{10,... | collective-permute-start | bytes 589832 | tf_op jit(solution)/shard_map/ppermute | solution.py:177
  17.9 1.4 %collective-permute-start.6 = (f32[200,128]{1,0:T(8,128)S(1)}, f32[200,128]{1,0:T(8,128)S(1)}, u32[]{:S(2)}, u32[]{:S(2)}) collective-permute-start(f32[200,128]{1,0:T(8,128)S(1)} %late.3), channel_id=1, source_target_pairs={{0,1},{1,0},{2,3},{3,2},{4,5},{5,4},{6,7},{7,6},{8,9},{9,8},{10,11... | collective-permute-start | bytes 307208 | tf_op jit(solution)/shard_map/ppermute | solution.py:196

commit v7 on v6

--- a/solution.py
+++ b/solution.py
@@ -28,10 +28,14 @@
 
 
 def pack_kernel(queries_hbm, preconditioner_hbm, packed, queries, preconditioner, arrived):
+    part = queries.shape[1] // 4
     copies = [
-        pltpu.make_async_copy(queries_hbm, queries, arrived.at[0]),
-        pltpu.make_async_copy(preconditioner_hbm, preconditioner, arrived.at[1]),
+        pltpu.make_async_copy(
+            queries_hbm.at[:, pl.ds(i * part, part)], queries.at[:, pl.ds(i * part, part)], arrived.at[i]
+        )
+        for i in range(4)
     ]
+    copies.append(pltpu.make_async_copy(preconditioner_hbm, preconditioner, arrived.at[4]))
     for copy in copies:
         copy.start()
     for copy in copies:
@@ -163,7 +167,7 @@
         scratch=[
             pltpu.VMEM(queries.shape, queries.dtype),
             pltpu.VMEM((1, width), jnp.float32),
-            pltpu.SemaphoreType.DMA((2,)),
+            pltpu.SemaphoreType.DMA((5,)),
         ],
     )
     across = lax.ppermute(packed, BOTH, by_core(6, 4))

time: 20.1 us -> 20.1 us (level)
  no operation moved by 1% of the time
where the time goes in v7:
time: 20.1 us; the launch traced here: 19.9 us
  starting transfers between devices  10.4 us (52%)
  Pallas kernels  5.24 us (26%)
  waiting for transfers between devices  4.2 us (21%)
    pallas_call x7, Pallas kernels, call(): pl.pallas_call(kernel, out_shape=out, in_specs=[anywhere() if hbm else vm...  5.24 us
    ppermute x1, starting transfers between devices, by_squares(): across = lax.ppermute(packed, BOTH, by_core(6, 4))  5.11 us
    ppermute x1, starting transfers between devices, by_squares(): pair = lax.ppermute(two, BOTH, by_core(1, 2))  2.03 us
    ppermute x1, starting transfers between devices, by_squares(): n2 = lax.ppermute(packed, BOTH, by_core(1, 2))  1.49 us
    ppermute x1, waiting for transfers between devices, by_squares(): corner = lax.ppermute(packed, BOTH, by_core(5, 7))  1.27 us
    ppermute x1, waiting for transfers between devices, by_squares(): pair = lax.ppermute(two, BOTH, by_core(1, 2))  1.22 us
    ppermute x1, starting transfers between devices, by_squares(): a1 = lax.ppermute(across, BOTH, by_core(2, 1))  1.13 us
    ppermute x1, waiting for transfers between devices, by_squares(): across = lax.ppermute(packed, BOTH, by_core(6, 4))  0.81 us
  transfers between devices with their start and end apart: 7, of which 5 were waited for; matrix products, arithmetic and copies ran while one was open for 0% of the time, Pallas kernels for 13%

profile of v7, /device:TPU:0, one launch (start us, length us, event | category | flops | bytes accessed | tf_op | source)
XLA Modules:
  0.0 19.9 jit_solution(13572877009381773281)
XLA Ops:
  0.0 0.0 copy-start
  0.0 1.0 %pack.1.rest_0_ = bf16[8,6144]{1,0:T(8,128)(2,1)S(1)} custom-call(bf16[12,4096]{1,0:T(8,128)(2,1)} %queries_hbm.1, f32[1,4096]{1,0:T(1,128)} %bitcast.1), custom_call_target="tpu_custom_call" | custom-call | flops 1000000000 | bytes 4194304 | tf_op jit(solution)/shard_map/pack/pallas_call | solution.py:137
  1.0 5.1 %collective-permute-start.2 = (bf16[8,6144]{1,0:T(8,128)(2,1)S(1)}, bf16[8,6144]{1,0:T(8,128)(2,1)S(1)}, u32[]{:S(2)}, u32[]{:S(2)}) collective-permute-start(bf16[8,6144]{1,0:T(8,128)(2,1)S(1)} %pack.1.rest_0_), channel_id=1, source_target_pairs={{0,12},{1,9},{2,14},{3,11},{4,8},{5,13},{6,10},{7,15},{8,4},{9,1},... | collective-permute-start | bytes 294920 | tf_op jit(solution)/shard_map/ppermute | solution.py:173
  6.2 0.0 collective-permute-start.4
  6.2 1.5 %collective-permute-start = (bf16[8,6144]{1,0:T(8,128)(2,1)S(1)}, bf16[8,6144]{1,0:T(8,128)(2,1)S(1)}, u32[]{:S(2)}, u32[]{:S(2)}) collective-permute-start(bf16[8,6144]{1,0:T(8,128)(2,1)S(1)} %pack.1.rest_0_), channel_id=1, source_target_pairs={{0,2},{1,5},{2,0},{3,7},{4,6},{5,1},{6,4},{7,3},{8,10},{9,13},{10,... | collective-permute-start | bytes 294920 | tf_op jit(solution)/shard_map/ppermute | solution.py:175
  7.6 0.6 %collective-permute-start.1 = (bf16[8,6144]{1,0:T(8,128)(2,1)S(1)}, bf16[8,6144]{1,0:T(8,128)(2,1)S(1)}, u32[]{:S(2)}, u32[]{:S(2)}) collective-permute-start(bf16[8,6144]{1,0:T(8,128)(2,1)S(1)} %pack.1.rest_0_), channel_id=1, source_target_pairs={{0,10},{1,15},{2,8},{3,13},{4,14},{5,11},{6,12},{7,9},{8,2},{9,7},... | collective-permute-start | bytes 294920 | tf_op jit(solution)/shard_map/ppermute | solution.py:176
  8.3 0.0 copy-done
  8.3 0.7 %squares.1 = f32[384,1]{1,0:T(8,128)S(1)} custom-call(bf16[384,4096]{1,0:T(8,128)(2,1)S(1)} %copy-done), custom_call_target="tpu_custom_call" | custom-call | flops 20000000000 | bytes 4194304 | tf_op jit(solution)/shard_map/squares/pallas_call | solution.py:137
  9.0 0.8 %collective-permute-done.2.second = bf16[8,6144]{1,0:T(8,128)(2,1)S(1)} collective-permute-done((bf16[8,6144]{1,0:T(8,128)(2,1)S(1)}, bf16[8,6144]{1,0:T(8,128)(2,1)S(1)}, u32[]{:S(2)}, u32[]{:S(2)}) %collective-permute-start.2) | collective-permute-done | bytes 98336 | tf_op jit(solution)/shard_map/ppermute | solution.py:173
  9.8 1.1 %collective-permute-start.3 = (bf16[8,6144]{1,0:T(8,128)(2,1)S(1)}, bf16[8,6144]{1,0:T(8,128)(2,1)S(1)}, u32[]{:S(2)}, u32[]{:S(2)}) collective-permute-start(bf16[8,6144]{1,0:T(8,128)(2,1)S(1)} %collective-permute-done.2.second), channel_id=1, source_target_pairs={{0,4},{1,3},{2,6},{3,1},{4,0},{5,7},{6,2},{7,5},{8,12},{9,11},{10,... | collective-permute-start | bytes 294920 | tf_op jit(solution)/shard_map/ppermute | solution.py:179
  10.9 0.3 %collective-permute-done.4.first = bf16[8,6144]{1,0:T(8,128)(2,1)S(1)} collective-permute-done((bf16[8,6144]{1,0:T(8,128)(2,1)S(1)}, bf16[8,6144]{1,0:T(8,128)(2,1)S(1)}, u32[]{:S(2)}, u32[]{:S(2)}) %collective-permute-start.4) | collective-permute-done | bytes 98336 | tf_op jit(solution)/shard_map/ppermute | solution.py:174
  11.3 2.0 %collective-permute-start.5 = (bf16[16,6144]{1,0:T(8,128)(2,1)S(1)}, bf16[16,6144]{1,0:T(8,128)(2,1)S(1)}, u32[]{:S(2)}, u32[]{:S(2)}) collective-permute-start(bf16[16,6144]{1,0:T(8,128)(2,1)S(1)} %join.1.rest_1_), channel_id=1, source_target_pairs={{0,2},{1,5},{2,0},{3,7},{4,6},{5,1},{6,4},{7,3},{8,10},{9,13},{10,... | collective-permute-start | bytes 589832 | tf_op jit(solution)/shard_map/ppermute | solution.py:181
  13.3 1.2 %early.1 = (f32[384,128]{1,0:T(8,128)S(1)}, f32[8,128]{1,0:T(8,128)S(1)}) custom-call(bf16[384,4096]{1,0:T(8,128)(2,1)S(1)} %copy-done, f32[384,1]{1,0:T(8,128)S(1)} %squares.1, bf16[8,6144]{1,0:T(8,128)(2,1)S(1)} %pack.1.rest_0_, bf16[16,6144]{1,0:T(8,128)(2,1)S(1)} %join.1.rest_1_), custom_call_target="tpu_custom_call" | custom-call | flops 20000000000 | bytes 4194304 | tf_op jit(solution)/shard_map/early/pallas_call | solution.py:137
  14.5 0.0 collective-permute-done.rest_0_
  14.5 1.3 %collective-permute-done.1.rest_1_ = bf16[8,6144]{1,0:T(8,128)(2,1)S(1)} collective-permute-done((bf16[8,6144]{1,0:T(8,128)(2,1)S(1)}, bf16[8,6144]{1,0:T(8,128)(2,1)S(1)}, u32[]{:S(2)}, u32[]{:S(2)}) %collective-permute-start.1) | collective-permute-done | bytes 98336 | tf_op jit(solution)/shard_map/ppermute | solution.py:176
  15.8 0.0 collective-permute-done.3.rest_2_
  15.8 1.2 %collective-permute-done.5.rest_3_ = bf16[16,6144]{1,0:T(8,128)(2,1)S(1)} collective-permute-done((bf16[16,6144]{1,0:T(8,128)(2,1)S(1)}, bf16[16,6144]{1,0:T(8,128)(2,1)S(1)}, u32[]{:S(2)}, u32[]{:S(2)}) %collective-permute-start.5) | collective-permute-done | bytes 196640 | tf_op jit(solution)/shard_map/ppermute | solution.py:181
  17.0 0.8 %late.3 = f32[200,128]{1,0:T(8,128)S(1)} custom-call(bf16[384,4096]{1,0:T(8,128)(2,1)S(1)} %copy-done, bf16[8,6144]{1,0:T(8,128)(2,1)S(1)} %collective-permute-done.rest_0_, bf16[8,6144]{1,0:T(8,128)(2,1)S(1)} %collective-permute-done.1.rest_1_, bf16[8,6144]{1,0:T(8,128)(2,1)S(1)} %collective-permute-done.3.rest_2_, ...), custom_call_target="tpu_custom_call" | custom-call | flops 1000000000 | bytes 4194304 | tf_op jit(solution)/shard_map/late/pallas_call | solution.py:137
  17.8 0.1 collective-permute-start.6
  17.9 0.8 %late.2.keep = f32[200,128]{1,0:T(8,128)S(1)} custom-call(bf16[384,4096]{1,0:T(8,128)(2,1)S(1)} %copy-done, bf16[8,6144]{1,0:T(8,128)(2,1)S(1)} %collective-permute-done.rest_0_, bf16[8,6144]{1,0:T(8,128)(2,1)S(1)} %collective-permute-done.1.rest_1_, bf16[8,6144]{1,0:T(8,128)(2,1)S(1)} %collective-permute-done.3.rest_2_, ...), custom_call_target="tpu_custom_call" | custom-call | flops 1000000000 | bytes 4194304 | tf_op jit(solution)/shard_map/late/pallas_call | solution.py:137
  18.7 0.5 %collective-permute-done.6.got = f32[200,128]{1,0:T(8,128)S(1)} collective-permute-done((f32[200,128]{1,0:T(8,128)S(1)}, f32[200,128]{1,0:T(8,128)S(1)}, u32[]{:S(2)}, u32[]{:S(2)}) %collective-permute-start.6) | collective-permute-done | bytes 102432 | tf_op jit(solution)/shard_map/ppermute | solution.py:200
  19.2 0.7 %finish.1 = f32[192,96]{1,0:T(8,128)} custom-call(f32[200,128]{1,0:T(8,128)S(1)} %late.2.keep, f32[200,128]{1,0:T(8,128)S(1)} %collective-permute-done.6.got), custom_call_target="tpu_custom_call" | custom-call | flops 1000000000 | bytes 4194304 | tf_op jit(solution)/shard_map/finish/pallas_call | solution.py:137
  (1 shorter events, 0.0 us)
Async XLA Ops:
  0.0 8.3 %copy-start = (bf16[384,4096]{1,0:T(8,128)(2,1)S(1)}, bf16[384,4096]{1,0:T(8,128)(2,1)}, u32[]{:S(2)}) copy-start(bf16[384,4096]{1,0:T(8,128)(2,1)} %documents.7) | copy-start | bytes 9437188
  1.0 8.7 %collective-permute-start.2 = (bf16[8,6144]{1,0:T(8,128)(2,1)S(1)}, bf16[8,6144]{1,0:T(8,128)(2,1)S(1)}, u32[]{:S(2)}, u32[]{:S(2)}) collective-permute-start(bf16[8,6144]{1,0:T(8,128)(2,1)S(1)} %pack.1.rest_0_), channel_id=1, source_target_pairs={{0,12},{1,9},{2,14},{3,11},{4,8},{5,13},{6,10},{7,15},{8,4},{9,1},... | collective-permute-start | bytes 294920 | tf_op jit(solution)/shard_map/ppermute | solution.py:173
  6.2 5.1 %collective-permute-start.4 = (bf16[8,6144]{1,0:T(8,128)(2,1)S(1)}, bf16[8,6144]{1,0:T(8,128)(2,1)S(1)}, u32[]{:S(2)}, u32[]{:S(2)}) collective-permute-start(bf16[8,6144]{1,0:T(8,128)(2,1)S(1)} %pack.1.rest_0_), channel_id=1, source_target_pairs={{0,4},{1,3},{2,6},{3,1},{4,0},{5,7},{6,2},{7,5},{8,12},{9,11},{10,... | collective-permute-start | bytes 294920 | tf_op jit(solution)/shard_map/ppermute | solution.py:174
  6.2 8.3 %collective-permute-start = (bf16[8,6144]{1,0:T(8,128)(2,1)S(1)}, bf16[8,6144]{1,0:T(8,128)(2,1)S(1)}, u32[]{:S(2)}, u32[]{:S(2)}) collective-permute-start(bf16[8,6144]{1,0:T(8,128)(2,1)S(1)} %pack.1.rest_0_), channel_id=1, source_target_pairs={{0,2},{1,5},{2,0},{3,7},{4,6},{5,1},{6,4},{7,3},{8,10},{9,13},{10,... | collective-permute-start | bytes 294920 | tf_op jit(solution)/shard_map/ppermute | solution.py:175
  7.6 8.1 %collective-permute-start.1 = (bf16[8,6144]{1,0:T(8,128)(2,1)S(1)}, bf16[8,6144]{1,0:T(8,128)(2,1)S(1)}, u32[]{:S(2)}, u32[]{:S(2)}) collective-permute-start(bf16[8,6144]{1,0:T(8,128)(2,1)S(1)} %pack.1.rest_0_), channel_id=1, source_target_pairs={{0,10},{1,15},{2,8},{3,13},{4,14},{5,11},{6,12},{7,9},{8,2},{9,7},... | collective-permute-start | bytes 294920 | tf_op jit(solution)/shard_map/ppermute | solution.py:176
  9.8 6.0 %collective-permute-start.3 = (bf16[8,6144]{1,0:T(8,128)(2,1)S(1)}, bf16[8,6144]{1,0:T(8,128)(2,1)S(1)}, u32[]{:S(2)}, u32[]{:S(2)}) collective-permute-start(bf16[8,6144]{1,0:T(8,128)(2,1)S(1)} %collective-permute-done.2.second), channel_id=1, source_target_pairs={{0,4},{1,3},{2,6},{3,1},{4,0},{5,7},{6,2},{7,5},{8,12},{9,11},{10,... | collective-permute-start | bytes 294920 | tf_op jit(solution)/shard_map/ppermute | solution.py:179
  11.3 5.8 %collective-permute-start.5 = (bf16[16,6144]{1,0:T(8,128)(2,1)S(1)}, bf16[16,6144]{1,0:T(8,128)(2,1)S(1)}, u32[]{:S(2)}, u32[]{:S(2)}) collective-permute-start(bf16[16,6144]{1,0:T(8,128)(2,1)S(1)} %join.1.rest_1_), channel_id=1, source_target_pairs={{0,2},{1,5},{2,0},{3,7},{4,6},{5,1},{6,4},{7,3},{8,10},{9,13},{10,... | collective-permute-start | bytes 589832 | tf_op jit(solution)/shard_map/ppermute | solution.py:181
  17.8 1.4 %collective-permute-start.6 = (f32[200,128]{1,0:T(8,128)S(1)}, f32[200,128]{1,0:T(8,128)S(1)}, u32[]{:S(2)}, u32[]{:S(2)}) collective-permute-start(f32[200,128]{1,0:T(8,128)S(1)} %late.3), channel_id=1, source_target_pairs={{0,1},{1,0},{2,3},{3,2},{4,5},{5,4},{6,7},{7,6},{8,9},{9,8},{10,11... | collective-permute-start | bytes 307208 | tf_op jit(solution)/shard_map/ppermute | solution.py:200

commit v8 on v7

--- a/solution.py
+++ b/solution.py
@@ -28,14 +28,14 @@
 
 
 def pack_kernel(queries_hbm, preconditioner_hbm, packed, queries, preconditioner, arrived):
-    part = queries.shape[1] // 4
+    part = queries.shape[1] // 2
     copies = [
         pltpu.make_async_copy(
             queries_hbm.at[:, pl.ds(i * part, part)], queries.at[:, pl.ds(i * part, part)], arrived.at[i]
         )
-        for i in range(4)
+        for i in range(2)
     ]
-    copies.append(pltpu.make_async_copy(preconditioner_hbm, preconditioner, arrived.at[4]))
+    copies.append(pltpu.make_async_copy(preconditioner_hbm, preconditioner, arrived.at[2]))
     for copy in copies:
         copy.start()
     for copy in copies:
@@ -167,7 +167,7 @@
         scratch=[
             pltpu.VMEM(queries.shape, queries.dtype),
             pltpu.VMEM((1, width), jnp.float32),
-            pltpu.SemaphoreType.DMA((5,)),
+            pltpu.SemaphoreType.DMA((3,)),
         ],
     )
     across = lax.ppermute(packed, BOTH, by_core(6, 4))

time: 20.1 us -> 20.1 us (level)
  no operation moved by 1% of the time
where the time goes in v8:
time: 20.1 us; the launch traced here: 20 us
  starting transfers between devices  10.4 us (52%)
  Pallas kernels  5.28 us (26%)
  waiting for transfers between devices  4.19 us (21%)
    pallas_call x7, Pallas kernels, call(): pl.pallas_call(kernel, out_shape=out, in_specs=[anywhere() if hbm else vm...  5.28 us
    ppermute x1, starting transfers between devices, by_squares(): across = lax.ppermute(packed, BOTH, by_core(6, 4))  5.11 us
    ppermute x1, starting transfers between devices, by_squares(): pair = lax.ppermute(two, BOTH, by_core(1, 2))  2.03 us
    ppermute x1, starting transfers between devices, by_squares(): n2 = lax.ppermute(packed, BOTH, by_core(1, 2))  1.49 us
    ppermute x1, waiting for transfers between devices, by_squares(): corner = lax.ppermute(packed, BOTH, by_core(5, 7))  1.27 us
    ppermute x1, waiting for transfers between devices, by_squares(): pair = lax.ppermute(two, BOTH, by_core(1, 2))  1.22 us
    ppermute x1, starting transfers between devices, by_squares(): a1 = lax.ppermute(across, BOTH, by_core(2, 1))  1.13 us
    ppermute x1, waiting for transfers between devices, by_squares(): across = lax.ppermute(packed, BOTH, by_core(6, 4))  0.81 us
  transfers between devices with their start and end apart: 7, of which 5 were waited for; matrix products, arithmetic and copies ran while one was open for 0% of the time, Pallas kernels for 13%

profile of v8, /device:TPU:0, one launch (start us, length us, event | category | flops | bytes accessed | tf_op | source)
XLA Modules:
  0.0 20.0 jit_solution(14871342251699151610)
XLA Ops:
  0.0 0.0 copy-start
  0.0 1.1 %pack.1.rest_0_ = bf16[8,6144]{1,0:T(8,128)(2,1)S(1)} custom-call(bf16[12,4096]{1,0:T(8,128)(2,1)} %queries_hbm.1, f32[1,4096]{1,0:T(1,128)} %bitcast.1), custom_call_target="tpu_custom_call" | custom-call | flops 1000000000 | bytes 4194304 | tf_op jit(solution)/shard_map/pack/pallas_call | solution.py:137
  1.1 5.1 %collective-permute-start.2 = (bf16[8,6144]{1,0:T(8,128)(2,1)S(1)}, bf16[8,6144]{1,0:T(8,128)(2,1)S(1)}, u32[]{:S(2)}, u32[]{:S(2)}) collective-permute-start(bf16[8,6144]{1,0:T(8,128)(2,1)S(1)} %pack.1.rest_0_), channel_id=1, source_target_pairs={{0,12},{1,9},{2,14},{3,11},{4,8},{5,13},{6,10},{7,15},{8,4},{9,1},... | collective-permute-start | bytes 294920 | tf_op jit(solution)/shard_map/ppermute | solution.py:173
  6.2 0.0 collective-permute-start.4
  6.2 1.5 %collective-permute-start = (bf16[8,6144]{1,0:T(8,128)(2,1)S(1)}, bf16[8,6144]{1,0:T(8,128)(2,1)S(1)}, u32[]{:S(2)}, u32[]{:S(2)}) collective-permute-start(bf16[8,6144]{1,0:T(8,128)(2,1)S(1)} %pack.1.rest_0_), channel_id=1, source_target_pairs={{0,2},{1,5},{2,0},{3,7},{4,6},{5,1},{6,4},{7,3},{8,10},{9,13},{10,... | collective-permute-start | bytes 294920 | tf_op jit(solution)/shard_map/ppermute | solution.py:175
  7.7 0.6 %collective-permute-start.1 = (bf16[8,6144]{1,0:T(8,128)(2,1)S(1)}, bf16[8,6144]{1,0:T(8,128)(2,1)S(1)}, u32[]{:S(2)}, u32[]{:S(2)}) collective-permute-start(bf16[8,6144]{1,0:T(8,128)(2,1)S(1)} %pack.1.rest_0_), channel_id=1, source_target_pairs={{0,10},{1,15},{2,8},{3,13},{4,14},{5,11},{6,12},{7,9},{8,2},{9,7},... | collective-permute-start | bytes 294920 | tf_op jit(solution)/shard_map/ppermute | solution.py:176
  8.3 0.0 copy-done
  8.3 0.7 %squares.1 = f32[384,1]{1,0:T(8,128)S(1)} custom-call(bf16[384,4096]{1,0:T(8,128)(2,1)S(1)} %copy-done), custom_call_target="tpu_custom_call" | custom-call | flops 20000000000 | bytes 4194304 | tf_op jit(solution)/shard_map/squares/pallas_call | solution.py:137
  9.0 0.8 %collective-permute-done.2.second = bf16[8,6144]{1,0:T(8,128)(2,1)S(1)} collective-permute-done((bf16[8,6144]{1,0:T(8,128)(2,1)S(1)}, bf16[8,6144]{1,0:T(8,128)(2,1)S(1)}, u32[]{:S(2)}, u32[]{:S(2)}) %collective-permute-start.2) | collective-permute-done | bytes 98336 | tf_op jit(solution)/shard_map/ppermute | solution.py:173
  9.8 1.1 %collective-permute-start.3 = (bf16[8,6144]{1,0:T(8,128)(2,1)S(1)}, bf16[8,6144]{1,0:T(8,128)(2,1)S(1)}, u32[]{:S(2)}, u32[]{:S(2)}) collective-permute-start(bf16[8,6144]{1,0:T(8,128)(2,1)S(1)} %collective-permute-done.2.second), channel_id=1, source_target_pairs={{0,4},{1,3},{2,6},{3,1},{4,0},{5,7},{6,2},{7,5},{8,12},{9,11},{10,... | collective-permute-start | bytes 294920 | tf_op jit(solution)/shard_map/ppermute | solution.py:179
  10.9 0.3 %collective-permute-done.4.first = bf16[8,6144]{1,0:T(8,128)(2,1)S(1)} collective-permute-done((bf16[8,6144]{1,0:T(8,128)(2,1)S(1)}, bf16[8,6144]{1,0:T(8,128)(2,1)S(1)}, u32[]{:S(2)}, u32[]{:S(2)}) %collective-permute-start.4) | collective-permute-done | bytes 98336 | tf_op jit(solution)/shard_map/ppermute | solution.py:174
  11.3 2.0 %collective-permute-start.5 = (bf16[16,6144]{1,0:T(8,128)(2,1)S(1)}, bf16[16,6144]{1,0:T(8,128)(2,1)S(1)}, u32[]{:S(2)}, u32[]{:S(2)}) collective-permute-start(bf16[16,6144]{1,0:T(8,128)(2,1)S(1)} %join.1.rest_1_), channel_id=1, source_target_pairs={{0,2},{1,5},{2,0},{3,7},{4,6},{5,1},{6,4},{7,3},{8,10},{9,13},{10,... | collective-permute-start | bytes 589832 | tf_op jit(solution)/shard_map/ppermute | solution.py:181
  13.3 1.2 %early.1 = (f32[384,128]{1,0:T(8,128)S(1)}, f32[8,128]{1,0:T(8,128)S(1)}) custom-call(bf16[384,4096]{1,0:T(8,128)(2,1)S(1)} %copy-done, f32[384,1]{1,0:T(8,128)S(1)} %squares.1, bf16[8,6144]{1,0:T(8,128)(2,1)S(1)} %pack.1.rest_0_, bf16[16,6144]{1,0:T(8,128)(2,1)S(1)} %join.1.rest_1_), custom_call_target="tpu_custom_call" | custom-call | flops 20000000000 | bytes 4194304 | tf_op jit(solution)/shard_map/early/pallas_call | solution.py:137
  14.5 0.0 collective-permute-done.rest_0_
  14.5 1.3 %collective-permute-done.1.rest_1_ = bf16[8,6144]{1,0:T(8,128)(2,1)S(1)} collective-permute-done((bf16[8,6144]{1,0:T(8,128)(2,1)S(1)}, bf16[8,6144]{1,0:T(8,128)(2,1)S(1)}, u32[]{:S(2)}, u32[]{:S(2)}) %collective-permute-start.1) | collective-permute-done | bytes 98336 | tf_op jit(solution)/shard_map/ppermute | solution.py:176
  15.8 0.0 collective-permute-done.3.rest_2_
  15.9 1.2 %collective-permute-done.5.rest_3_ = bf16[16,6144]{1,0:T(8,128)(2,1)S(1)} collective-permute-done((bf16[16,6144]{1,0:T(8,128)(2,1)S(1)}, bf16[16,6144]{1,0:T(8,128)(2,1)S(1)}, u32[]{:S(2)}, u32[]{:S(2)}) %collective-permute-start.5) | collective-permute-done | bytes 196640 | tf_op jit(solution)/shard_map/ppermute | solution.py:181
  17.1 0.8 %late.3 = f32[200,128]{1,0:T(8,128)S(1)} custom-call(bf16[384,4096]{1,0:T(8,128)(2,1)S(1)} %copy-done, bf16[8,6144]{1,0:T(8,128)(2,1)S(1)} %collective-permute-done.rest_0_, bf16[8,6144]{1,0:T(8,128)(2,1)S(1)} %collective-permute-done.1.rest_1_, bf16[8,6144]{1,0:T(8,128)(2,1)S(1)} %collective-permute-done.3.rest_2_, ...), custom_call_target="tpu_custom_call" | custom-call | flops 1000000000 | bytes 4194304 | tf_op jit(solution)/shard_map/late/pallas_call | solution.py:137
  17.9 0.1 collective-permute-start.6
  17.9 0.8 %late.2.keep = f32[200,128]{1,0:T(8,128)S(1)} custom-call(bf16[384,4096]{1,0:T(8,128)(2,1)S(1)} %copy-done, bf16[8,6144]{1,0:T(8,128)(2,1)S(1)} %collective-permute-done.rest_0_, bf16[8,6144]{1,0:T(8,128)(2,1)S(1)} %collective-permute-done.1.rest_1_, bf16[8,6144]{1,0:T(8,128)(2,1)S(1)} %collective-permute-done.3.rest_2_, ...), custom_call_target="tpu_custom_call" | custom-call | flops 1000000000 | bytes 4194304 | tf_op jit(solution)/shard_map/late/pallas_call | solution.py:137
  18.7 0.5 %collective-permute-done.6.got = f32[200,128]{1,0:T(8,128)S(1)} collective-permute-done((f32[200,128]{1,0:T(8,128)S(1)}, f32[200,128]{1,0:T(8,128)S(1)}, u32[]{:S(2)}, u32[]{:S(2)}) %collective-permute-start.6) | collective-permute-done | bytes 102432 | tf_op jit(solution)/shard_map/ppermute | solution.py:200
  19.2 0.7 %finish.1 = f32[192,96]{1,0:T(8,128)} custom-call(f32[200,128]{1,0:T(8,128)S(1)} %late.2.keep, f32[200,128]{1,0:T(8,128)S(1)} %collective-permute-done.6.got), custom_call_target="tpu_custom_call" | custom-call | flops 1000000000 | bytes 4194304 | tf_op jit(solution)/shard_map/finish/pallas_call | solution.py:137
  (1 shorter events, 0.0 us)
Async XLA Ops:
  0.0 8.3 %copy-start = (bf16[384,4096]{1,0:T(8,128)(2,1)S(1)}, bf16[384,4096]{1,0:T(8,128)(2,1)}, u32[]{:S(2)}) copy-start(bf16[384,4096]{1,0:T(8,128)(2,1)} %documents.7) | copy-start | bytes 9437188
  1.1 8.7 %collective-permute-start.2 = (bf16[8,6144]{1,0:T(8,128)(2,1)S(1)}, bf16[8,6144]{1,0:T(8,128)(2,1)S(1)}, u32[]{:S(2)}, u32[]{:S(2)}) collective-permute-start(bf16[8,6144]{1,0:T(8,128)(2,1)S(1)} %pack.1.rest_0_), channel_id=1, source_target_pairs={{0,12},{1,9},{2,14},{3,11},{4,8},{5,13},{6,10},{7,15},{8,4},{9,1},... | collective-permute-start | bytes 294920 | tf_op jit(solution)/shard_map/ppermute | solution.py:173
  6.2 5.1 %collective-permute-start.4 = (bf16[8,6144]{1,0:T(8,128)(2,1)S(1)}, bf16[8,6144]{1,0:T(8,128)(2,1)S(1)}, u32[]{:S(2)}, u32[]{:S(2)}) collective-permute-start(bf16[8,6144]{1,0:T(8,128)(2,1)S(1)} %pack.1.rest_0_), channel_id=1, source_target_pairs={{0,4},{1,3},{2,6},{3,1},{4,0},{5,7},{6,2},{7,5},{8,12},{9,11},{10,... | collective-permute-start | bytes 294920 | tf_op jit(solution)/shard_map/ppermute | solution.py:174
  6.2 8.3 %collective-permute-start = (bf16[8,6144]{1,0:T(8,128)(2,1)S(1)}, bf16[8,6144]{1,0:T(8,128)(2,1)S(1)}, u32[]{:S(2)}, u32[]{:S(2)}) collective-permute-start(bf16[8,6144]{1,0:T(8,128)(2,1)S(1)} %pack.1.rest_0_), channel_id=1, source_target_pairs={{0,2},{1,5},{2,0},{3,7},{4,6},{5,1},{6,4},{7,3},{8,10},{9,13},{10,... | collective-permute-start | bytes 294920 | tf_op jit(solution)/shard_map/ppermute | solution.py:175
  7.7 8.1 %collective-permute-start.1 = (bf16[8,6144]{1,0:T(8,128)(2,1)S(1)}, bf16[8,6144]{1,0:T(8,128)(2,1)S(1)}, u32[]{:S(2)}, u32[]{:S(2)}) collective-permute-start(bf16[8,6144]{1,0:T(8,128)(2,1)S(1)} %pack.1.rest_0_), channel_id=1, source_target_pairs={{0,10},{1,15},{2,8},{3,13},{4,14},{5,11},{6,12},{7,9},{8,2},{9,7},... | collective-permute-start | bytes 294920 | tf_op jit(solution)/shard_map/ppermute | solution.py:176
  9.8 6.0 %collective-permute-start.3 = (bf16[8,6144]{1,0:T(8,128)(2,1)S(1)}, bf16[8,6144]{1,0:T(8,128)(2,1)S(1)}, u32[]{:S(2)}, u32[]{:S(2)}) collective-permute-start(bf16[8,6144]{1,0:T(8,128)(2,1)S(1)} %collective-permute-done.2.second), channel_id=1, source_target_pairs={{0,4},{1,3},{2,6},{3,1},{4,0},{5,7},{6,2},{7,5},{8,12},{9,11},{10,... | collective-permute-start | bytes 294920 | tf_op jit(solution)/shard_map/ppermute | solution.py:179
  11.3 5.8 %collective-permute-start.5 = (bf16[16,6144]{1,0:T(8,128)(2,1)S(1)}, bf16[16,6144]{1,0:T(8,128)(2,1)S(1)}, u32[]{:S(2)}, u32[]{:S(2)}) collective-permute-start(bf16[16,6144]{1,0:T(8,128)(2,1)S(1)} %join.1.rest_1_), channel_id=1, source_target_pairs={{0,2},{1,5},{2,0},{3,7},{4,6},{5,1},{6,4},{7,3},{8,10},{9,13},{10,... | collective-permute-start | bytes 589832 | tf_op jit(solution)/shard_map/ppermute | solution.py:181
  17.9 1.4 %collective-permute-start.6 = (f32[200,128]{1,0:T(8,128)S(1)}, f32[200,128]{1,0:T(8,128)S(1)}, u32[]{:S(2)}, u32[]{:S(2)}) collective-permute-start(f32[200,128]{1,0:T(8,128)S(1)} %late.3), channel_id=1, source_target_pairs={{0,1},{1,0},{2,3},{3,2},{4,5},{5,4},{6,7},{7,6},{8,9},{9,8},{10,11... | collective-permute-start | bytes 307208 | tf_op jit(solution)/shard_map/ppermute | solution.py:200
